TPU v7x, 256 devices: a whole 4x4x8 slice. The times are simulated.
256 devices in a mesh: dp: 16 (over y, x_hi, core), seq: 16 (over x_lo, z).
Axes of the slice: x: 4 (x_hi: 2, x_lo: 2; x = x_hi * 2 + x_lo), y: 4, z: 8, core: 2. Of those that a mesh axis runs over, the one named last changes fastest.
Arguments:
- proj_inputs: bfloat16 [16, 2048, 2560], P('dp', 'seq'), may hold values from -6 to 6
- queries: bfloat16 [16, 2048, 4096], P('dp', 'seq'), may hold values from -140 to 140
- key_state_rows: bfloat16 [16, 2048, 512], P('dp', 'seq'), may hold values from -5 to 5
- value_state_rows: bfloat16 [16, 2048, 512], P('dp', 'seq'), may hold values from -6 to 6
- d_out: bfloat16 [16, 2048, 4096], P('dp', 'seq'), may hold values from -6 to 6
- w_tiles: bfloat16 [320, 128, 128], P('seq', 'dp'), may hold values from -0.15625 to 0.15625
- tile_rows: int32 [32, 10], replicated, may hold values from 0 to 19, as said below
- loss_scale: int32 [1], replicated, may hold values from 64 to 256
Outputs:
- d_x: bfloat16 [16, 2048, 2560], P('dp', 'seq')
- d_k: bfloat16 [16, 2048, 512], P('dp', 'seq')
- d_v: bfloat16 [16, 2048, 512], P('dp', 'seq')
- d_w: float32 [320, 128, 128], P('seq', 'dp')
Inputs may be any that keep to these rules, and one draw needn't show every extreme that they name: `tile_rows`: each row lists 10 distinct row tiles out of 20, in increasing order.
All inputs are finite; a program needn't handle non-finite values.
Results may differ from a plain program's by a relative error of at most 0.035.
Values may be sent and summed in bfloat16 or wider, within the bound.
A program may use at most 128 MiB of HBM per device.

v0:
```python
import math

import jax
import jax.numpy as jnp
from jax import lax
from jax.sharding import PartitionSpec as P

D = 2560
QUERY_HEADS = 32
KEY_VALUE_HEADS = 4
HEAD_WIDTH = 128
TILE = 128
KEEP = 10
RTILES = 20
NCB = 32


def tile_terms(grad_cols, tiles, row_ids):
    picker = (row_ids[:, :, None] == jnp.arange(RTILES, dtype=jnp.int32)[None, None, :]).astype(
        jnp.bfloat16
    )
    dense_part = jnp.einsum(
        "ckr,ckij->ricj", picker, tiles, preferred_element_type=jnp.float32
    ).astype(jnp.bfloat16)
    return jnp.einsum("tcj,ricj->tri", grad_cols, dense_part, preferred_element_type=jnp.float32)


def fold_tiles(total, grad_blocks, tiles, row_table, group_size):
    group_size = math.gcd(tiles.shape[0], group_size)
    count = tiles.shape[0] // group_size

    def one_group(group_idx, running):
        col_off = group_idx * group_size
        tile_part = lax.dynamic_slice_in_dim(tiles, col_off, group_size, 0)
        grad_part = lax.dynamic_slice_in_dim(grad_blocks, col_off, group_size, 1)
        row_part = lax.dynamic_slice_in_dim(row_table, col_off, group_size, 0)
        terms = tile_terms(grad_part, tile_part, row_part)
        return running + terms

    return lax.fori_loop(0, count, one_group, total)


def body(
    proj_inputs, queries, key_state_rows, value_state_rows, d_out, w_tiles, tile_rows, loss_scale
):
    sequence_count = lax.axis_size("seq")
    token_rows = proj_inputs.shape[1]
    length = token_rows * sequence_count
    local_heads = QUERY_HEADS // sequence_count
    head_copies = sequence_count // KEY_VALUE_HEADS
    block_step = NCB // sequence_count
    softmax_scale = HEAD_WIDTH ** (-0.5)
    q_split = queries[0].reshape(token_rows, sequence_count, local_heads * HEAD_WIDTH)
    grad_split = d_out[0].reshape(token_rows, sequence_count, local_heads * HEAD_WIDTH)
    k_split = jnp.broadcast_to(
        key_state_rows[0].reshape(token_rows, KEY_VALUE_HEADS, 1, HEAD_WIDTH),
        (token_rows, KEY_VALUE_HEADS, head_copies, HEAD_WIDTH),
    ).reshape(token_rows, sequence_count, HEAD_WIDTH)
    v_split = jnp.broadcast_to(
        value_state_rows[0].reshape(token_rows, KEY_VALUE_HEADS, 1, HEAD_WIDTH),
        (token_rows, KEY_VALUE_HEADS, head_copies, HEAD_WIDTH),
    ).reshape(token_rows, sequence_count, HEAD_WIDTH)
    query_head_rows, k_head, v_head, output_grad_heads = (
        lax.all_to_all(q_split, "seq", split_axis=1, concat_axis=0, tiled=True),
        lax.all_to_all(k_split, "seq", split_axis=1, concat_axis=0, tiled=True),
        lax.all_to_all(v_split, "seq", split_axis=1, concat_axis=0, tiled=True),
        lax.all_to_all(grad_split, "seq", split_axis=1, concat_axis=0, tiled=True),
    )
    query_head_rows = query_head_rows.reshape(length, local_heads, HEAD_WIDTH)
    output_grad_heads = output_grad_heads.reshape(length, local_heads, HEAD_WIDTH)
    k_head = k_head.reshape(length, HEAD_WIDTH)
    v_head = v_head.reshape(length, HEAD_WIDTH)
    block_count = max(1, min(8, length // 256))
    block_rows = length // block_count
    dk_total = jnp.zeros((length, HEAD_WIDTH), jnp.float32)
    dv_total = jnp.zeros((length, HEAD_WIDTH), jnp.float32)
    dq_pieces = []
    for block_idx in range(block_count):
        row_first = block_idx * block_rows
        limit = row_first + block_rows
        q_block = query_head_rows[row_first:limit]
        grad_block = output_grad_heads[row_first:limit]
        k_known = k_head[:limit]
        v_known = v_head[:limit]
        scores = (
            jnp.einsum("qnd,kd->nqk", q_block, k_known, preferred_element_type=jnp.float32)
            * softmax_scale
        )
        query_pos = row_first + jnp.arange(block_rows, dtype=jnp.int32)[:, None]
        key_pos = jnp.arange(limit, dtype=jnp.int32)[None, :]
        scores = jnp.where((key_pos <= query_pos)[None], scores, -1e30)
        row_top = jnp.max(scores, axis=-1, keepdims=True)
        expo = jnp.exp(scores - row_top)
        probs = expo / jnp.sum(expo, axis=-1, keepdims=True)
        probs_low = probs.astype(jnp.bfloat16)
        dprobs = jnp.einsum("qnd,kd->nqk", grad_block, v_known, preferred_element_type=jnp.float32)
        row_delta = jnp.sum(probs_low.astype(jnp.float32) * dprobs, axis=-1, keepdims=True)
        dscores = (probs * (dprobs - row_delta)).astype(jnp.bfloat16)
        dq_block = (
            jnp.einsum("nqk,kd->qnd", dscores, k_known, preferred_element_type=jnp.float32)
            * softmax_scale
        )
        dq_pieces.append(dq_block.astype(jnp.bfloat16))
        dk_total = dk_total.at[:limit].add(
            jnp.einsum("nqk,qnd->kd", dscores, q_block, preferred_element_type=jnp.float32)
            * softmax_scale
        )
        dv_total = dv_total.at[:limit].add(
            jnp.einsum("nqk,qnd->kd", probs_low, grad_block, preferred_element_type=jnp.float32)
        )
    dq_heads = jnp.concatenate(dq_pieces, axis=0).reshape(length, local_heads * HEAD_WIDTH)
    dq_tokens = lax.all_to_all(dq_heads, "seq", split_axis=0, concat_axis=1, tiled=True)
    key_grad_parts, value_grad_parts = (
        lax.all_to_all(dk_total, "seq", split_axis=0, concat_axis=1, tiled=True),
        lax.all_to_all(dv_total, "seq", split_axis=0, concat_axis=1, tiled=True),
    )
    d_k = (
        key_grad_parts.reshape(token_rows, KEY_VALUE_HEADS, head_copies, HEAD_WIDTH)
        .sum(axis=2)
        .reshape(1, token_rows, KEY_VALUE_HEADS * HEAD_WIDTH)
        .astype(jnp.bfloat16)
    )
    d_v = (
        value_grad_parts.reshape(token_rows, KEY_VALUE_HEADS, head_copies, HEAD_WIDTH)
        .sum(axis=2)
        .reshape(1, token_rows, KEY_VALUE_HEADS * HEAD_WIDTH)
        .astype(jnp.bfloat16)
    )
    grad_blocks = dq_tokens.reshape(token_rows, NCB, TILE)
    empty = jnp.zeros((token_rows, RTILES, TILE), jnp.float32)
    row_gathered = lax.all_gather(w_tiles, "dp", axis=1, tiled=True)
    portion = lax.all_gather(row_gathered, "seq", axis=0, tiled=True)
    blocks = portion.shape[0] // KEEP
    dx_total = fold_tiles(
        empty, grad_blocks, portion.reshape(blocks, KEEP, TILE, TILE), tile_rows, block_step
    )
    d_x = dx_total.reshape(1, token_rows, D).astype(jnp.bfloat16)
    col_start = lax.axis_index("seq") * block_step
    my_rows = lax.dynamic_slice_in_dim(tile_rows, col_start, block_step, 0).reshape(
        block_step * KEEP
    )
    dq_local = dq_heads.reshape(length, block_step, TILE)
    portion = lax.all_gather(proj_inputs[0], "seq", axis=0, tiled=True)
    piece_rows = math.gcd(portion.shape[0], token_rows)
    pieces = portion.shape[0] // piece_rows

    def one_piece(piece_idx, running):
        rows_x = lax.dynamic_slice_in_dim(portion, piece_idx * piece_rows, piece_rows, 0).reshape(
            piece_rows, RTILES, TILE
        )
        picked = jnp.take(rows_x, my_rows, axis=1).reshape(piece_rows, block_step, KEEP, TILE)
        grad_rows = lax.dynamic_slice_in_dim(dq_local, piece_idx * piece_rows, piece_rows, 0)
        return running + jnp.einsum(
            "tcki,tcj->ckij", picked, grad_rows, preferred_element_type=jnp.float32
        )

    grads = lax.fori_loop(
        0, pieces, one_piece, jnp.zeros((block_step, KEEP, TILE, TILE), jnp.float32)
    )
    summed = lax.psum_scatter(
        grads.reshape(block_step * KEEP, TILE, TILE).astype(jnp.bfloat16),
        "dp",
        scatter_dimension=1,
        tiled=True,
    ).astype(jnp.float32)
    d_w = summed / loss_scale[0].astype(jnp.float32)
    return (d_x, d_k, d_v, d_w)


def solution(mesh):
    placed = (
        P("dp", "seq", None),
        P("dp", "seq", None),
        P("dp", "seq", None),
        P("dp", "seq", None),
        P("dp", "seq", None),
        P("seq", "dp", None),
        P(),
        P(),
    )
    return jax.shard_map(
        body,
        mesh=mesh,
        in_specs=placed,
        out_specs=(
            P("dp", "seq", None),
            P("dp", "seq", None),
            P("dp", "seq", None),
            P("seq", "dp", None),
        ),
        check_vma=False,
    )
```

profile of v0, /device:TPU:2, one launch (start us, length us, event | category | flops | bytes accessed | tf_op | source)
XLA Modules:
  0.0 510.7 jit_solution(13424898685550500001)
XLA Ops:
  11.3 9.9 %all-to-all-start = ((bf16[128,16,128]{2,0,1:T(8,128)(2,1)}), bf16[128,16,128]{2,0,1:T(8,128)(2,1)S(1)}, u32[]{:S(2)}, u32[]{:S(2)}) async-start(bf16[128,16,128]{2,0,1:T(8,128)(2,1)} %bitcast), calls=%async_computation | async-start | bytes 1048576 | tf_op jit(solution)/shard_map/all_to_all | solution.py:65
  21.3 19.3 %all-to-all-done = bf16[128,16,128]{2,0,1:T(8,128)(2,1)S(1)} async-done(((bf16[128,16,128]{2,0,1:T(8,128)(2,1)}), bf16[128,16,128]{2,0,1:T(8,128)(2,1)S(1)}, u32[]{:S(2)}, u32[]{:S(2)}) %all-to-all-start) | async-done | bytes 524320 | tf_op jit(solution)/shard_map/all_to_all | solution.py:65
  41.5 5.4 %all-to-all-start.2 = ((bf16[128,16,128]{2,0,1:T(8,128)(2,1)}), bf16[128,16,128]{2,0,1:T(8,128)(2,1)S(1)}, u32[]{:S(2)}, u32[]{:S(2)}) async-start(bf16[128,16,128]{2,0,1:T(8,128)(2,1)} %bitcast.8), calls=%async_computation.2 | async-start | bytes 1048576 | tf_op jit(solution)/shard_map/all_to_all | solution.py:66
  48.5 18.0 %all-to-all-done.2 = bf16[128,16,128]{2,0,1:T(8,128)(2,1)S(1)} async-done(((bf16[128,16,128]{2,0,1:T(8,128)(2,1)}), bf16[128,16,128]{2,0,1:T(8,128)(2,1)S(1)}, u32[]{:S(2)}, u32[]{:S(2)}) %all-to-all-start.2) | async-done | bytes 524320 | tf_op jit(solution)/shard_map/all_to_all | solution.py:66
  66.5 4.7 all-to-all-start.1
  71.3 32.3 %all_gather.9 = bf16[20,128,128]{2,1,0:T(8,128)(2,1)} all-gather(bf16[20,8,128]{2,1,0:T(8,128)(2,1)S(1)} %copy-done.58), channel_id=1, replica_groups=mesh['dp'=16,'seq'=16] {'dp'}, dimensions={1}, use_global_device_ids=true | all-gather | bytes 696320 | tf_op jit(solution)/shard_map/all_gather | solution.py:131
  111.2 15.4 %all-to-all-start.3 = ((bf16[128,16,256]{2,0,1:T(8,128)(2,1)}), bf16[128,16,256]{2,0,1:T(8,128)(2,1)}, u32[]{:S(2)}, u32[]{:S(2)}) async-start(bf16[128,16,256]{2,0,1:T(8,128)(2,1)} %copy.142), calls=%async_computation.3 | async-start | bytes 2097152 | tf_op jit(solution)/shard_map/all_to_all | solution.py:67
  143.3 20.0 %all-to-all-done.3 = bf16[128,16,256]{2,0,1:T(8,128)(2,1)} async-done(((bf16[128,16,256]{2,0,1:T(8,128)(2,1)}), bf16[128,16,256]{2,0,1:T(8,128)(2,1)}, u32[]{:S(2)}, u32[]{:S(2)}) %all-to-all-start.3) | async-done | bytes 1048608 | tf_op jit(solution)/shard_map/all_to_all | solution.py:67
  163.4 2.2 fusion.264
  184.6 3.0 fusion.97
  187.7 3.5 fusion.271
  191.2 3.0 fusion.92
  194.1 3.8 fusion.274
  197.9 3.2 fusion.87
  201.1 4.1 fusion.277
  205.3 3.6 fusion.43
  208.8 4.6 fusion.280
  213.4 3.9 fusion.56
  217.3 16.5 %exponential_reduce_fusion = (f32[2,256]{1,0:T(2,128)}, f32[2,256,1792]{1,2,0:T(8,128)}) fusion(bf16[1792,128,1]{1,0,2:T(8,128)(2,1)} %bitcast.573, pred[256,1792]{0,1:T(8,128)(4,1)} %iota_compare_fusion.2, bf16[256,2,128]{2,1,0:T(2,128)(2,1)} %slice.519), kind=kOutput, calls=%fused_computation.56 | convolution fusion | flops 238552832 | bytes 4720640 | tf_op jit(solution)/shard_map/sub | solution.py:93
  233.9 4.3 fusion.58
  238.1 5.0 fusion.285
  243.1 4.3 fusion.59
  247.4 4.7 all-to-all-start.6
  277.1 13.4 %all-to-all-done.6 = f32[16,128,128]{2,1,0:T(8,128)} async-done(((f32[16,128,128]{2,1,0:T(8,128)}), f32[16,128,128]{2,1,0:T(8,128)}, u32[]{:S(2)}, u32[]{:S(2)}) %all-to-all-start.6) | async-done | bytes 1048608 | tf_op jit(solution)/shard_map/all_to_all | solution.py:115
  290.5 5.6 %all-to-all-start.5 = ((f32[16,128,128]{2,1,0:T(8,128)}), f32[16,128,128]{2,1,0:T(8,128)}, u32[]{:S(2)}, u32[]{:S(2)}) async-start(f32[16,128,128]{2,1,0:T(8,128)} %bitcast.558), calls=%async_computation.5 | async-start | bytes 2097152 | tf_op jit(solution)/shard_map/all_to_all | solution.py:114
  297.1 2.3 fusion.118
  299.5 2.4 fusion.122
  311.4 22.7 %all-to-all-done.5 = f32[16,128,128]{2,1,0:T(8,128)} async-done(((f32[16,128,128]{2,1,0:T(8,128)}), f32[16,128,128]{2,1,0:T(8,128)}, u32[]{:S(2)}, u32[]{:S(2)}) %all-to-all-start.5) | async-done | bytes 1048608 | tf_op jit(solution)/shard_map/all_to_all | solution.py:114
  334.1 5.6 %all-to-all-start.4 = ((bf16[16,128,256]{1,2,0:T(8,128)(2,1)}), bf16[16,128,256]{1,2,0:T(8,128)(2,1)}, u32[]{:S(2)}, u32[]{:S(2)}) async-start(bf16[16,128,256]{1,2,0:T(8,128)(2,1)} %copy.167), calls=%async_computation.4 | async-start | bytes 2097152 | tf_op jit(solution)/shard_map/all_to_all | solution.py:112
  342.9 86.2 %while.47 = (s32[]{:T(128)}, f32[2,10,128,128]{3,2,1,0:T(8,128)}, s32[20]{0:T(128)S(1)}, bf16[2048,2560]{0,1:T(8,128)(2,1)}, bf16[2048,2,128]{2,0,1:T(8,128)(2,1...) while((s32[]{:T(128)}, f32[2,10,128,128]{3,2,1,0:T(8,128)}, s32[20]{0:T(128)S(1)}, ...), condition=%wide.region_29.30_spmd.clone, body=%wide.region_28.29_spmd.clone.sunk | while | flops 84870328 | bytes 8590069 | solution.py:157
  345.5 2.3 convolution_add_fusion.2
  350.4 2.8 convolution_add_fusion.2
  355.8 2.8 convolution_add_fusion.2
  361.2 2.8 convolution_add_fusion.2
  366.7 2.8 convolution_add_fusion.2
  372.1 2.8 convolution_add_fusion.2
  377.5 2.8 convolution_add_fusion.2
  382.9 2.8 convolution_add_fusion.2
  388.4 2.8 convolution_add_fusion.2
  393.8 2.8 convolution_add_fusion.2
  399.2 2.8 convolution_add_fusion.2
  404.7 2.8 convolution_add_fusion.2
  410.1 2.8 convolution_add_fusion.2
  415.5 2.8 convolution_add_fusion.2
  420.9 2.8 convolution_add_fusion.2
  426.3 2.8 convolution_add_fusion.2
  432.1 56.8 %while.46 = (s32[]{:T(128)}, f32[128,20,128]{2,0,1:T(8,128)S(1)}, bf16[128,32,128]{0,2,1:T(8,128)(2,1)}, bf16[32,10,128,128]{3,2,1,0:T(8,128)(2,1)}, s32[32,10]{...) while((s32[]{:T(128)}, f32[128,20,128]{2,0,1:T(8,128)S(1)}, ...), condition=%wide.region_25.26_spmd.clone, body=%wide.region_24.25_spmd.clone.sunk | while | flops 182190480 | bytes 7274897 | solution.py:40
  490.3 12.2 %reduce-scatter.4.cloned.1.call-done = bf16[8,2560]{1,0:T(8,128)(2,1)} async-done(((bf16[128,2560]{1,0:T(8,128)(2,1)}), bf16[8,2560]{1,0:T(8,128)(2,1)}) %reduce-scatter.4.cloned.1.call-update) | async-done | bytes 40976
  (456 shorter events, 190.3 us)
Async XLA Ops:
  7.2 14.1 %copy-start.47 = (bf16[1,128,512]{2,1,0:T(8,128)(2,1)S(1)}, bf16[1,128,512]{2,1,0:T(8,128)(2,1)}, u32[]{:S(2)}) copy-start(bf16[1,128,512]{2,1,0:T(8,128)(2,1)} %param.51) | copy-start | bytes 393220
  7.2 335.7 %all-gather.6.cloned.1.call-start = ((), (), s32[]{:S(2)}) async-start(), calls=%async_computation.9 | async-start | bytes 11141120 | tf_op jit(solution)/shard_map/all_gather | solution.py:143
  10.4 36.5 %copy-start.17 = (bf16[1,128,4096]{2,1,0:T(8,128)(2,1)S(1)}, bf16[1,128,4096]{2,1,0:T(8,128)(2,1)}, u32[]{:S(2)}) copy-start(bf16[1,128,4096]{2,1,0:T(8,128)(2,1)} %param.49) | copy-start | bytes 3145732
  11.3 29.3 %all-to-all-start = ((bf16[128,16,128]{2,0,1:T(8,128)(2,1)}), bf16[128,16,128]{2,0,1:T(8,128)(2,1)S(1)}, u32[]{:S(2)}, u32[]{:S(2)}) async-start(bf16[128,16,128]{2,0,1:T(8,128)(2,1)} %bitcast), calls=%async_computation | async-start | bytes 1048576 | tf_op jit(solution)/shard_map/all_to_all | solution.py:65
  41.5 25.0 %all-to-all-start.2 = ((bf16[128,16,128]{2,0,1:T(8,128)(2,1)}), bf16[128,16,128]{2,0,1:T(8,128)(2,1)S(1)}, u32[]{:S(2)}, u32[]{:S(2)}) async-start(bf16[128,16,128]{2,0,1:T(8,128)(2,1)} %bitcast.8), calls=%async_computation.2 | async-start | bytes 1048576 | tf_op jit(solution)/shard_map/all_to_all | solution.py:66
  47.1 24.1 %copy-start.58 = (bf16[20,8,128]{2,1,0:T(8,128)(2,1)S(1)}, bf16[20,8,128]{2,1,0:T(8,128)(2,1)}, u32[]{:S(2)}) copy-start(bf16[20,8,128]{2,1,0:T(8,128)(2,1)} %param.53) | copy-start | bytes 122884
  66.5 44.7 %all-to-all-start.1 = ((bf16[128,16,256]{2,0,1:T(8,128)(2,1)}), bf16[128,16,256]{2,0,1:T(8,128)(2,1)S(1)}, u32[]{:S(2)}, u32[]{:S(2)}) async-start(bf16[128,16,256]{2,0,1:T(8,128)(2,1)} %copy.139), calls=%async_computation.1 | async-start | bytes 2097152 | tf_op jit(solution)/shard_map/all_to_all | solution.py:64
  71.2 360.8 %all-gather.4.cloned.1.call-start = ((), (), s32[]{:S(2)}) async-start(), calls=%async_computation.8 | async-start | bytes 11141120 | tf_op jit(solution)/shard_map/all_gather | solution.py:132
  103.6 2.8 copy-start.59
  111.2 52.2 %all-to-all-start.3 = ((bf16[128,16,256]{2,0,1:T(8,128)(2,1)}), bf16[128,16,256]{2,0,1:T(8,128)(2,1)}, u32[]{:S(2)}, u32[]{:S(2)}) async-start(bf16[128,16,256]{2,0,1:T(8,128)(2,1)} %copy.142), calls=%async_computation.3 | async-start | bytes 2097152 | tf_op jit(solution)/shard_map/all_to_all | solution.py:67
  141.7 25.6 %copy-start.25 = (bf16[2,128,1,256]{3,1,0,2:T(8,128)(2,1)S(1)}, bf16[2,128,1,256]{3,1,0,2:T(8,128)(2,1)}, u32[]{:S(2)}) copy-start(bf16[2,128,1,256]{3,1,0,2:T(8,128)(2,1)} %get-tuple-element.491) | copy-start | bytes 393220
  141.7 27.9 %copy-start.24 = (bf16[2,128,1,256]{3,1,0,2:T(8,128)(2,1)S(1)}, bf16[2,128,1,256]{3,1,0,2:T(8,128)(2,1)}, u32[]{:S(2)}) copy-start(bf16[2,128,1,256]{3,1,0,2:T(8,128)(2,1)} %get-tuple-element.490) | copy-start | bytes 393220
  141.7 30.2 %copy-start.23 = (bf16[2,128,1,256]{3,1,0,2:T(8,128)(2,1)S(1)}, bf16[2,128,1,256]{3,1,0,2:T(8,128)(2,1)}, u32[]{:S(2)}) copy-start(bf16[2,128,1,256]{3,1,0,2:T(8,128)(2,1)} %get-tuple-element.489) | copy-start | bytes 393220
  141.7 32.5 %copy-start.22 = (bf16[2,128,1,256]{3,1,0,2:T(8,128)(2,1)S(1)}, bf16[2,128,1,256]{3,1,0,2:T(8,128)(2,1)}, u32[]{:S(2)}) copy-start(bf16[2,128,1,256]{3,1,0,2:T(8,128)(2,1)} %get-tuple-element.488) | copy-start | bytes 393220
  163.4 13.1 %copy-start.21 = (bf16[2,128,1,256]{3,1,0,2:T(8,128)(2,1)S(1)}, bf16[2,128,1,256]{3,1,0,2:T(8,128)(2,1)}, u32[]{:S(2)}) copy-start(bf16[2,128,1,256]{3,1,0,2:T(8,128)(2,1)} %get-tuple-element.487) | copy-start | bytes 393220
  165.6 13.6 %copy-start.20 = (bf16[2,128,1,256]{3,1,0,2:T(8,128)(2,1)S(1)}, bf16[2,128,1,256]{3,1,0,2:T(8,128)(2,1)}, u32[]{:S(2)}) copy-start(bf16[2,128,1,256]{3,1,0,2:T(8,128)(2,1)} %get-tuple-element.485) | copy-start | bytes 393220
  167.9 9.2 %copy-start.26 = (bf16[2,128,1,256]{3,1,0,2:T(8,128)(2,1)S(1)}, bf16[2,128,1,256]{3,1,0,2:T(8,128)(2,1)}, u32[]{:S(2)}) copy-start(bf16[2,128,1,256]{3,1,0,2:T(8,128)(2,1)} %get-tuple-element.495) | copy-start | bytes 393220
  170.2 9.7 %copy-start.30 = (bf16[256,2,128]{2,1,0:T(2,128)(2,1)S(1)}, bf16[256,2,128]{2,1,0:T(2,128)(2,1)}, u32[]{:S(2)}) copy-start(bf16[256,2,128]{2,1,0:T(2,128)(2,1)} %slice.471) | copy-start | bytes 393220
  177.8 3.3 copy-start.56
  184.6 69.4 %copy-start.16 = (f32[2,256,512]{1,2,0:T(8,128)}, f32[2,256,512]{1,2,0:T(8,128)S(1)}, u32[]{:S(2)}) copy-start(f32[2,256,512]{1,2,0:T(8,128)S(1)} %get-tuple-element.506) | copy-start | bytes 3145732
  247.4 43.1 %all-to-all-start.6 = ((f32[16,128,128]{2,1,0:T(8,128)}), f32[16,128,128]{2,1,0:T(8,128)}, u32[]{:S(2)}, u32[]{:S(2)}) async-start(f32[16,128,128]{2,1,0:T(8,128)} %bitcast.565), calls=%async_computation.6 | async-start | bytes 2097152 | tf_op jit(solution)/shard_map/all_to_all | solution.py:115
  252.1 1.9 copy-start.51
  252.1 1.9 copy-start.55
  252.1 1.9 copy-start.65
  259.8 2.0 copy-start.9
  261.9 2.2 copy-start.11
  262.8 2.3 copy-start.6
  265.1 2.7 copy-start.10
  266.0 2.7 copy-start.4
  266.0 1.9 copy-start.49
  266.0 1.9 copy-start.68
  268.8 2.5 copy-start.48
  269.6 3.0 copy-start.8
  269.6 3.0 copy-start.60
  277.1 19.0 %copy-start.29 = (bf16[4,128,1,128]{3,1,0,2:T(8,128)(2,1)S(1)}, bf16[4,128,1,128]{3,1,0,2:T(8,128)(2,1)}, u32[]{:S(2)}) copy-start(bf16[4,128,1,128]{3,1,0,2:T(8,128)(2,1)} %slice.546) | copy-start | bytes 393220
  277.1 20.0 %copy-start.44 = (bf16[6,128,1,128]{3,1,0,2:T(8,128)(2,1)S(1)}, bf16[6,128,1,128]{3,1,0,2:T(8,128)(2,1)}, u32[]{:S(2)}) copy-start(bf16[6,128,1,128]{3,1,0,2:T(8,128)(2,1)} %slice.550) | copy-start | bytes 589828
  277.1 22.4 %copy-start.42 = (bf16[8,128,1,128]{3,1,0,2:T(8,128)(2,1)S(1)}, bf16[8,128,1,128]{3,1,0,2:T(8,128)(2,1)}, u32[]{:S(2)}) copy-start(bf16[8,128,1,128]{3,1,0,2:T(8,128)(2,1)} %slice.554) | copy-start | bytes 786436
  290.5 43.5 %all-to-all-start.5 = ((f32[16,128,128]{2,1,0:T(8,128)}), f32[16,128,128]{2,1,0:T(8,128)}, u32[]{:S(2)}, u32[]{:S(2)}) async-start(f32[16,128,128]{2,1,0:T(8,128)} %bitcast.558), calls=%async_computation.5 | async-start | bytes 2097152 | tf_op jit(solution)/shard_map/all_to_all | solution.py:114
  296.1 5.7 %copy-start.7 = (bf16[2,256,1280]{1,2,0:T(8,128)(2,1)S(1)}, bf16[2,256,1280]{1,2,0:T(8,128)(2,1)}, u32[]{:S(2)}) copy-start(bf16[2,256,1280]{1,2,0:T(8,128)(2,1)} %copy-done.6) | copy-start | bytes 3932164
  296.1 5.7 %copy-start.40 = (bf16[10,128,1,128]{3,1,0,2:T(8,128)(2,1)S(1)}, bf16[10,128,1,128]{3,1,0,2:T(8,128)(2,1)}, u32[]{:S(2)}) copy-start(bf16[10,128,1,128]{3,1,0,2:T(8,128)(2,1)} %slice.558) | copy-start | bytes 983044
  297.1 5.9 %copy-start.5 = (bf16[2,256,1536]{1,2,0:T(8,128)(2,1)S(1)}, bf16[2,256,1536]{1,2,0:T(8,128)(2,1)}, u32[]{:S(2)}) copy-start(bf16[2,256,1536]{1,2,0:T(8,128)(2,1)} %copy-done.4) | copy-start | bytes 4718596
  297.1 5.9 %copy-start.38 = (bf16[12,128,1,128]{3,1,0,2:T(8,128)(2,1)S(1)}, bf16[12,128,1,128]{3,1,0,2:T(8,128)(2,1)}, u32[]{:S(2)}) copy-start(bf16[12,128,1,128]{3,1,0,2:T(8,128)(2,1)} %slice.562) | copy-start | bytes 1179652
  301.9 2.5 copy-start.3
  301.9 2.5 copy-start.36
  303.1 2.6 copy-start.1
  311.4 31.5 %copy-start.69 = (s32[20]{0:T(128)S(1)}, s32[20]{0:T(128)}, u32[]{:S(2)}) copy-start(s32[20]{0:T(128)} %reshape.761) | copy-start | bytes 244
  334.1 97.9 %all-to-all-start.4 = ((bf16[16,128,256]{1,2,0:T(8,128)(2,1)}), bf16[16,128,256]{1,2,0:T(8,128)(2,1)}, u32[]{:S(2)}, u32[]{:S(2)}) async-start(bf16[16,128,256]{1,2,0:T(8,128)(2,1)} %copy.167), calls=%async_computation.4 | async-start | bytes 2097152 | tf_op jit(solution)/shard_map/all_to_all | solution.py:112
  339.7 162.8 %reduce-scatter.4.cloned.1.call-start = ((), (), s32[]{:S(2)}) async-start(), calls=%async_computation.10 | async-start | bytes 696320
  (32 other events, 48.1 us)
Sparse Core Ops, SparseCore 0:
  10.3 208.0 all-gather.5
  220.2 189.7 all-gather.3
  432.1 70.2 reduce-scatter.3
where the time goes:
time: 519 us; the launch traced here: 511 us
  matrix products  170 us (33%)
  local copies, waits for them, and re-layouts  117 us (23%)
  waiting for transfers between devices  106 us (20%)
  starting transfers between devices  51.4 us (10%)
  blocking collectives  32.3 us (6%)
  other arithmetic  17.1 us (3%)
  between operations  15.5 us (3%)
    dot_general x16, matrix products, one_piece(): jnp.einsum('tcki,tcj->ckij', picked, grad_rows, preferred_element_type=jn...  44.5 us
    sub x8, matrix products, body(): expo = jnp.exp(scores - row_top)  40.8 us
    all_gather x1, blocking collectives, body(): row_gathered = lax.all_gather(w_tiles, 'dp', axis=1, tiled=True)  32.3 us
    dot_general x8, matrix products, body(): jnp.einsum('nqk,qnd->kd', probs_low, grad_block, preferred_element_type=j...  25.5 us
    dot_general x16, matrix products, tile_terms(): jnp.einsum('tcj,ricj->tri', grad_cols, dense_part, preferred_element_type...  25.3 us
    all_to_all x1, waiting for transfers between devices, body(): lax.all_to_all(dk_total, 'seq', split_axis=0, concat_axis=1, tiled=True)  22.7 us
    all_to_all x1, waiting for transfers between devices, body(): lax.all_to_all(grad_split, 'seq', split_axis=1, concat_axis=0, tiled=True)  20 us
    all_to_all x1, waiting for transfers between devices, body(): lax.all_to_all(k_split, 'seq', split_axis=1, concat_axis=0, tiled=True)  19.3 us
  transfers between devices with their start and end apart: 10, of which 6 were waited for; matrix products, arithmetic and copies ran while one was open for 57% of the time, Pallas kernels for 0%

commit v1 on v0

v1 whole, which is shorter than its diff:
```python
import functools

import jax
import jax.numpy as jnp
from jax import lax
from jax.experimental import pallas as pl
from jax.experimental.pallas import tpu as pltpu
from jax.sharding import PartitionSpec as P

D = 2560
W = 128
KEEP = 10
RTILES = 20
ZN = 8
HALF = 2048
HP = 4
R = HP * W
CK = 256
SCALE = W**-0.5
EXP_SCALE = SCALE * 1.4426950408889634
MESH = pl.DeviceIdType.MESH
F32 = jnp.float32
BF16 = jnp.bfloat16


def dot_t(a, b):
    return lax.dot_general(a, b, (((1,), (1,)), ((), ())), preferred_element_type=F32)


def dot(a, b):
    return lax.dot_general(a, b, (((1,), (0,)), ((), ())), preferred_element_type=F32)


def fold(x, op):
    return op(x.reshape(x.shape[0] // 8, 8, x.shape[1]), axis=0)


def attend(g, blk, head, z, qbuf, dobuf, kbuf, vbuf, kt, acc, e_scr, dp_scr, q_s, do_s, dq_t, dq_ref):
    for i in range(HP):
        cols = pl.ds(pl.multiple_of((head + i) * W, W), W)
        q_s[i * W : (i + 1) * W, :] = qbuf[blk, :, cols]
        do_s[i * W : (i + 1) * W, :] = dobuf[blk, :, cols]
    t = blk * ZN + z
    full = t // 2

    def chunk(ref, c):
        return ref[g, c // 4, pl.ds((c % 4) * 2, 2)].reshape(CK, W)

    def rows(c):
        return pl.ds(pl.multiple_of(c * CK, CK), CK)

    def scores(c, top):
        s = dot_t(chunk(kbuf, c), q_s[...])
        e_scr[rows(c), :] = s
        return jnp.maximum(top, fold(s, jnp.max))

    top = lax.fori_loop(0, full, scores, jnp.full((8, R), -1e30, F32))
    s = dot_t(chunk(kbuf, full), q_s[...])
    key = full * CK + lax.broadcasted_iota(jnp.int32, (CK, R), 0)
    pos = t * W + lax.broadcasted_iota(jnp.int32, (CK, R), 1) % W
    s = jnp.where(key <= pos, s, -1e30)
    e_scr[rows(full), :] = s
    top = jnp.max(jnp.maximum(top, fold(s, jnp.max)), axis=0, keepdims=True)

    def exps(c, carry):
        total, weighted = carry
        e = jnp.exp2((e_scr[rows(c), :] - top) * EXP_SCALE)
        dp = dot_t(chunk(vbuf, c), do_s[...])
        e_scr[rows(c), :] = e
        dp_scr[rows(c), :] = dp
        return total + fold(e, jnp.sum), weighted + fold(e * dp, jnp.sum)

    zero = jnp.zeros((8, R), F32)
    total, weighted = lax.fori_loop(0, full + 1, exps, (zero, zero))
    inv = 1.0 / jnp.sum(total, axis=0, keepdims=True)
    delta = jnp.sum(weighted, axis=0, keepdims=True) * inv
    dq_t[...] = jnp.zeros_like(dq_t)

    def grads(c, carry):
        p = e_scr[rows(c), :] * inv
        ds = (p * (dp_scr[rows(c), :] - delta)).astype(BF16)
        acc[0, g, rows(c), :] += dot(ds, q_s[...])
        acc[1, g, rows(c), :] += dot(p.astype(BF16), do_s[...])
        dq_t[...] += dot(kt[g, :, pl.ds(pl.multiple_of(c * CK, CK), CK)], ds)
        return carry

    lax.fori_loop(0, full + 1, grads, 0)
    for i in range(HP):
        cols = pl.ds(pl.multiple_of((head + i) * W, W), W)
        dq_ref[blk, :, cols] = (dq_t[:, i * W : (i + 1) * W] * SCALE).T.astype(BF16)


def attention_kernel(
    q_ref, do_ref, k_ref, v_ref, dq_ref, dk_ref, dv_ref,
    qbuf, dobuf, kbuf, vbuf, kt, acc, e_scr, dp_scr, q_s, do_s, dq_t,
    out_r, in_r, out_l, in_l, swap_out, swap_in,
    own_sem, kv_send, kv_recv, q_send, q_recv, ring_send, ring_recv,
    rs_send, rs_recv, swap_send, swap_recv,
):
    s = lax.axis_index("seq")
    h, z = s // ZN, s % ZN
    partner = (1 - h) * ZN + z
    right = h * ZN + (z + 1) % ZN
    left = h * ZN + (z + ZN - 1) % ZN
    barrier = pltpu.get_barrier_semaphore()
    for d in (partner, right, left):
        pl.semaphore_signal(barrier, inc=1, device_id={"seq": d}, device_id_type=MESH)
    pl.semaphore_wait(barrier, 3)

    def remote(src, dst, ssem, rsem, d):
        return pltpu.make_async_remote_copy(src, dst, ssem, rsem, device_id={"seq": d}, device_id_type=MESH)

    def cols(start, size):
        return pl.ds(pl.multiple_of(start, W), size)

    swaps, own = [], []
    for kv, (src, buf) in enumerate(((k_ref, kbuf), (v_ref, vbuf))):
        for g in range(2):
            swaps.append(
                remote(src.at[:, cols(((1 - h) * 2 + g) * W, W)], buf.at[g, h, z],
                       kv_send.at[kv, g], kv_recv.at[kv, g], partner))
            own.append(pltpu.make_async_copy(
                src.at[:, cols((h * 2 + g) * W, W)], buf.at[g, h, z], own_sem.at[kv, g]))
    for c in swaps:
        c.start()
    for c in own:
        c.start()
    q_copies, q_own = [], []
    for g in range(2):
        for i, (src, buf) in enumerate(((q_ref, qbuf), (do_ref, dobuf))):
            part = pl.ds(g * 1024, 1024)
            q_copies.append(remote(src.at[:, cols((1 - h) * HALF + g * 1024, 1024)], buf.at[h, :, part],
                                   q_send.at[g, i], q_recv.at[g, i], partner))
            q_own.append(pltpu.make_async_copy(
                src.at[:, cols(h * HALF + g * 1024, 1024)], buf.at[h, :, part], own_sem.at[2 + g, i]))
    for c in q_copies:
        c.start()
    for c in q_own:
        c.start()
    acc[...] = jnp.zeros_like(acc)

    def ring(kv, way, step):
        buf = (kbuf, vbuf)[kv]
        if way == 0:
            at, to = (z + ZN - step) % ZN, right
        else:
            at, to = (z + step) % ZN, left
        return remote(buf.at[:, :, at], buf.at[:, :, at], ring_send.at[kv, way, step], ring_recv.at[kv, way, step], to)

    hops = ((4, 3), (3, 4))
    for c in own:
        c.wait()
    for kv in range(2):
        for g in range(2):
            swaps[kv * 2 + g].wait_recv()
        for way in range(2):
            ring(kv, way, 0).start()
    for step in range(4):
        for kv in range(2):
            for way in range(2):
                if step < hops[kv][way]:
                    ring(kv, way, step).wait_recv()
                    if step + 1 < hops[kv][way]:
                        ring(kv, way, step + 1).start()

    def turn(b, carry):
        kt[b // 16, :, cols((b % 16) * W, W)] = kbuf[b // 16, (b % 16) // ZN, b % ZN].T
        return carry

    lax.fori_loop(0, 32, turn, 0)
    for c in q_own:
        c.wait()

    def package(g, d):
        return [[acc[kv, g, pl.ds(pl.multiple_of((hl * ZN + d) * W, W), W), :] * (SCALE if kv == 0 else 1.0)
                 for hl in range(2)] for kv in range(2)]

    def rs(g, way, step):
        src, dst, to = ((out_r, in_r, right), (out_l, in_l, left))[way]
        return remote(src.at[g, step], dst.at[g, step], rs_send.at[g, way, step], rs_recv.at[g, way, step], to)

    def rs_step(g, step):
        for way, n in ((0, 4), (1, 3)):
            if step >= n:
                continue
            src, dst = ((out_r, in_r), (out_l, in_l))[way]
            d = (z + 4 - step) % ZN if way == 0 else (z + ZN - 3 + step) % ZN
            part = package(g, d)
            if step > 0:
                rs(g, way, step - 1).wait_recv()
            for kv in range(2):
                for hl in range(2):
                    v = part[kv][hl]
                    if step > 0:
                        v = v + dst[g, step - 1, kv, hl].astype(F32)
                    src[g, step, kv, hl] = v.astype(BF16)
            rs(g, way, step).start()

    def pair(g):
        return remote(swap_out.at[g], swap_in.at[g], swap_send.at[g], swap_recv.at[g], partner)

    def rs_end(g):
        part = package(g, z)
        rs(g, 0, 3).wait_recv()
        rs(g, 1, 2).wait_recv()
        for kv, out in enumerate((dk_ref, dv_ref)):
            both = [part[kv][hl] + in_r[g, 3, kv, hl].astype(F32) + in_l[g, 2, kv, hl].astype(F32) for hl in range(2)]
            mine = jnp.where(h == 0, both[0], both[1])
            other = jnp.where(h == 0, both[1], both[0])
            out[:, cols((h * 2 + g) * W, W)] = mine.astype(BF16)
            swap_out[g, kv] = other.astype(BF16)
        pair(g).start()

    def rs_out(g):
        pair(g).wait_recv()
        for kv, out in enumerate((dk_ref, dv_ref)):
            out[:, cols(((1 - h) * 2 + g) * W, W)] = swap_in[g, kv]

    per_g = 16 // HP

    def work(it, carry):
        g = it // per_g
        rest = it % per_g
        second = rest // (per_g // 2)
        blk = jnp.where(second == 0, h, 1 - h)
        head = g * 8 + (rest % (per_g // 2)) * HP
        for gg in range(2):

            @pl.when(it == gg * per_g + per_g // 2)
            def _():
                for i in range(2):
                    q_copies[gg * 2 + i].wait_recv()

        for step in range(4):

            @pl.when(it == per_g + step)
            def _():
                rs_step(0, step)

        attend(g, blk, head, z, qbuf, dobuf, kbuf, vbuf, kt, acc, e_scr, dp_scr, q_s, do_s, dq_t, dq_ref)
        return carry

    lax.fori_loop(0, 2 * per_g, work, 0)
    rs_step(1, 0)
    rs_end(0)
    for step in range(1, 4):
        rs_step(1, step)
    rs_out(0)
    rs_end(1)
    rs_out(1)
    for c in swaps + q_copies:
        c.wait_send()
    for kv in range(2):
        for way in range(2):
            for step in range(hops[kv][way]):
                ring(kv, way, step).wait_send()
    for g in range(2):
        for way, n in ((0, 4), (1, 3)):
            for step in range(n):
                rs(g, way, step).wait_send()
        pair(g).wait_send()


def attention(q, do, k, v):
    any_spec = pl.BlockSpec(memory_space=pl.ANY)
    vmem = pl.BlockSpec(memory_space=pltpu.VMEM)
    dma = pltpu.SemaphoreType.DMA
    return pl.pallas_call(
        attention_kernel,
        out_shape=(
            jax.ShapeDtypeStruct((2, W, HALF), BF16),
            jax.ShapeDtypeStruct((W, 512), BF16),
            jax.ShapeDtypeStruct((W, 512), BF16),
        ),
        in_specs=[any_spec] * 4,
        out_specs=(vmem, vmem, vmem),
        scratch_shapes=[
            pltpu.VMEM((2, W, HALF), BF16),
            pltpu.VMEM((2, W, HALF), BF16),
            pltpu.VMEM((2, 2, ZN, W, W), BF16),
            pltpu.VMEM((2, 2, ZN, W, W), BF16),
            pltpu.VMEM((2, W, 2048), BF16),
            pltpu.VMEM((2, 2, 2048, W), F32),
            pltpu.VMEM((2048, R), F32),
            pltpu.VMEM((2048, R), F32),
            pltpu.VMEM((R, W), BF16),
            pltpu.VMEM((R, W), BF16),
            pltpu.VMEM((W, R), F32),
            pltpu.VMEM((2, 4, 2, 2, W, W), BF16),
            pltpu.VMEM((2, 4, 2, 2, W, W), BF16),
            pltpu.VMEM((2, 3, 2, 2, W, W), BF16),
            pltpu.VMEM((2, 3, 2, 2, W, W), BF16),
            pltpu.VMEM((2, 2, W, W), BF16),
            pltpu.VMEM((2, 2, W, W), BF16),
            dma((4, 2)),
            dma((2, 2)),
            dma((2, 2)),
            dma((2, 2)),
            dma((2, 2)),
            dma((2, 2, 4)),
            dma((2, 2, 4)),
            dma((2, 2, 4)),
            dma((2, 2, 4)),
            dma((2,)),
            dma((2,)),
        ],
        compiler_params=pltpu.CompilerParams(
            collective_id=0, has_side_effects=True, vmem_limit_bytes=48 * 2**20
        ),
        cost_estimate=pl.CostEstimate(flops=10 * 10**9, bytes_accessed=8 * 10**6, transcendentals=10**7),
    )(q, do, k, v)


def project_kernel(inv_ref, rows_ref, dq_ref, x_ref, w_ref, dx_ref, dw_ref, xt, wcat):
    for r in range(RTILES):
        xt[r] = x_ref[:, :, r * W : (r + 1) * W].reshape(2 * W, W).T

    def weights(c, carry):
        dq_c = dq_ref[:, :, pl.ds(pl.multiple_of(c * W, W), W)].reshape(2 * W, W)
        xs = jnp.concatenate([xt[rows_ref[c * KEEP + k]] for k in range(KEEP)], axis=0)
        out = dot(xs, dq_c).astype(BF16)
        dw_ref[pl.ds(c * KEEP, KEEP)] = out.reshape(KEEP, W, W)
        return carry

    lax.fori_loop(0, 16, weights, 0)

    def inputs(r2, carry):
        for i in range(2):
            for c in range(16):
                k = inv_ref[(r2 * 2 + i) * 16 + c]
                tile = w_ref[c * KEEP + jnp.minimum(k, KEEP - 1)]
                wcat[i * W : (i + 1) * W, c * W : (c + 1) * W] = jnp.where(k < KEEP, tile, jnp.zeros_like(tile))
        out = dot_t(dq_ref[...].reshape(2 * W, HALF), wcat[...]).astype(BF16)
        dx_ref[:, :, pl.ds(pl.multiple_of(r2 * 2 * W, 2 * W), 2 * W)] = out.reshape(2, W, 2 * W)
        return carry

    lax.fori_loop(0, RTILES // 2, inputs, 0)


def project(inv, rows, dq, x, w):
    vmem = pl.BlockSpec(memory_space=pltpu.VMEM)
    smem = pl.BlockSpec(memory_space=pltpu.SMEM)
    return pl.pallas_call(
        project_kernel,
        out_shape=(
            jax.ShapeDtypeStruct((2, W, D), BF16),
            jax.ShapeDtypeStruct((16 * KEEP, W, W), BF16),
        ),
        in_specs=[smem, smem, vmem, vmem, vmem],
        out_specs=(vmem, vmem),
        scratch_shapes=[
            pltpu.VMEM((RTILES, W, 2 * W), BF16),
            pltpu.VMEM((2 * W, HALF), BF16),
        ],
        compiler_params=pltpu.CompilerParams(vmem_limit_bytes=48 * 2**20),
        cost_estimate=pl.CostEstimate(flops=4 * 10**9, bytes_accessed=15 * 10**6, transcendentals=0),
    )(inv, rows, dq, x, w)


def body(x, q, k, v, do, w, tile_rows, loss_scale):
    s = lax.axis_index("seq")
    h = s // ZN
    halves = [list(range(ZN)), list(range(ZN, 2 * ZN))]
    cross = [(i, (i + ZN) % (2 * ZN)) for i in range(2 * ZN)]
    w_all = lax.all_gather(w, "dp", axis=1, tiled=True)
    w_half = lax.all_gather(w_all, "seq", axis=0, tiled=True, axis_index_groups=halves)
    x_other = lax.ppermute(x[0], "seq", cross)
    x_pair = jnp.where(h == 0, jnp.stack([x[0], x_other]), jnp.stack([x_other, x[0]]))
    my_rows = lax.dynamic_slice_in_dim(tile_rows, h * 16, 16, 0)
    hit = my_rows[:, :, None] == jnp.arange(RTILES, dtype=jnp.int32)
    inv = jnp.min(jnp.where(hit, jnp.arange(KEEP, dtype=jnp.int32)[None, :, None], KEEP), axis=1).T.reshape(-1)

    dq, dk, dv = attention(q[0], do[0], k[0], v[0])
    dx_pair, dw_part = project(inv, my_rows.reshape(-1), dq, x_pair, w_half)
    dx_mine = lax.dynamic_index_in_dim(dx_pair, h, 0, keepdims=False)
    dx_theirs = lax.dynamic_index_in_dim(dx_pair, 1 - h, 0, keepdims=False)
    dx_got = lax.ppermute(dx_theirs, "seq", cross)
    dx = (dx_mine.astype(F32) + dx_got.astype(F32)).astype(BF16)
    dw = lax.psum_scatter(dw_part, "dp", scatter_dimension=1, tiled=True)
    dw = lax.psum_scatter(dw, "seq", scatter_dimension=0, tiled=True, axis_index_groups=halves)
    dw = dw.astype(F32) / loss_scale[0].astype(F32)
    return dx[None], dk[None], dv[None], dw


def solution(mesh):
    tokens = P("dp", "seq", None)
    tiles = P("seq", "dp", None)
    return jax.shard_map(
        body,
        mesh=mesh,
        in_specs=(tokens,) * 5 + (tiles, P(), P()),
        out_specs=(tokens, tokens, tokens, tiles),
        check_vma=False,
    )
```

time: 519 us -> 335 us (0.65); the launches traced: 511 us -> 334 us
  matrix products: 170 us -> 0 us
  Pallas kernels: 0 us -> 146 us
  local copies, waits for them, and re-layouts: 117 us -> 17.4 us
  starting transfers between devices: 51.4 us -> 1.73 us
  waiting for transfers between devices: 106 us -> 123 us
  other arithmetic: 17.1 us -> 2.72 us
    pallas_call x0 -> x2, Pallas kernels: none -> 146 us  [the longest x1 130 us: attention(): pl.pallas_call(attention_kernel, out_shape=(jax.ShapeDtypeStruct((2, W, H...]
    dot_general x80 -> x0, matrix products: 130 us -> none  [the longest x16 44.5 us: one_piece(): jnp.einsum('tcki,tcj->ckij', picked, grad_rows, preferred_element_type=jn...]
    all_to_all x7 -> x0, waiting for transfers between devices: 93.4 us -> none  [the longest x1 22.7 us: body(): lax.all_to_all(dk_total, 'seq', split_axis=0, concat_axis=1, tiled=True)]
    unnamed x4, waiting for transfers between devices: 12.2 us -> 87.1 us
    all_to_all x7 -> x0, starting transfers between devices: 51.3 us -> none  [the longest x1 15.4 us: body(): lax.all_to_all(grad_split, 'seq', split_axis=1, concat_axis=0, tiled=True)]
    sub x8 -> x0, matrix products: 40.8 us -> none  [body(): expo = jnp.exp(scores - row_top)]
    dynamic_slice x50 -> x2, local copies, waits for them, and re-layouts: 36.7 us -> 0.16 us  [body(): my_rows = lax.dynamic_slice_in_dim(tile_rows, h * 16, 16, 0)]
    reduce_scatter x0 -> x1, waiting for transfers between devices: none -> 36.3 us  [body(): lax.psum_scatter(dw, 'seq', scatter_dimension=0, tiled=True, axis_index_g...]
  transfers between devices with their start and end apart: 10 -> 5, of which waited for: 6 -> 2; matrix products, arithmetic and copies ran while one was open for 57% -> 1% of each run, Pallas kernels for 0% -> 39%
where the time goes in v1:
time: 335 us; the launch traced here: 334 us
  Pallas kernels  146 us (44%)
  waiting for transfers between devices  123 us (37%)
  blocking collectives  27.9 us (8%)
  local copies, waits for them, and re-layouts  17.4 us (5%)
  between operations  14.6 us (4%)
    pallas_call x1, Pallas kernels, attention(): pl.pallas_call(attention_kernel, out_shape=(jax.ShapeDtypeStruct((2, W, H...  130 us
    unnamed x4, waiting for transfers between devices  87.1 us
    reduce_scatter x1, waiting for transfers between devices, body(): lax.psum_scatter(dw, 'seq', scatter_dimension=0, tiled=True, axis_index_g...  36.3 us
    all_gather x1, blocking collectives, body(): w_all = lax.all_gather(w, 'dp', axis=1, tiled=True)  27.9 us
    unnamed x22, local copies, waits for them, and re-layouts  16.9 us
    pallas_call x1, Pallas kernels, project(): pl.pallas_call(project_kernel, out_shape=(jax.ShapeDtypeStruct((2, W, D),...  15.9 us
  transfers between devices with their start and end apart: 5, of which 2 were waited for; matrix products, arithmetic and copies ran while one was open for 1% of the time, Pallas kernels for 39%

profile of v1, /device:TPU:2, one launch (start us, length us, event | category | flops | bytes accessed | tf_op | source)
XLA Modules:
  0.0 334.1 jit_solution(13585462143446874931)
XLA Ops:
  7.2 0.0 copy-start
  7.2 0.0 copy-start.1
  7.2 0.0 copy-start.3
  7.2 0.0 copy-start.4
  7.2 0.0 all-gather.2.cloned.1.call-start
  7.3 27.9 %all_gather.6 = bf16[20,128,128]{2,1,0:T(8,128)(2,1)} all-gather(bf16[20,8,128]{2,1,0:T(8,128)(2,1)} %param.13), channel_id=1, replica_groups=mesh['dp'=16,'seq'=16] {'dp'}, dimensions={1}, use_global_device_ids=true | all-gather | bytes 696320 | tf_op jit(solution)/shard_map/all_gather | solution.py:365
  35.2 0.0 all-gather.2.cloned.1.call-update
  35.2 0.0 reduce-scatter.7.cloned.1.call-start
  35.2 1.5 collective-permute-start
  36.8 0.0 copy-done
  36.8 0.1 constant_dynamic-slice_fusion
  36.8 0.1 copy.18
  36.9 0.1 select_reduce_fusion
  37.0 0.1 copy.17
  37.1 0.1 reshape.18.inv_ref
  37.2 0.1 reshape.19.rows_ref
  37.3 0.0 copy-done.1
  37.3 0.0 copy-done.3
  37.3 0.0 copy-done.4
  37.3 0.0 copy-start.2
  37.3 1.2 copy-done.2
  38.5 0.0 copy-start.7
  38.5 130.5 %shard_map.111 = (bf16[2,128,2048]{2,1,0:T(8,128)(2,1)S(1)}, bf16[128,512]{1,0:T(8,128)(2,1)S(1)}, bf16[128,512]{1,0:T(8,128)(2,1)S(1)}) custom-call(bf16[128,4096]{1,0:T(8,128)(2,1)S(1)} %bitcast.31, bf16[128,4096]{1,0:T(8,128)(2,1)S(1)} %bitcast.32, bf16[128,512]{1,0:T(8,128)(2,1)S(1)} %bitcast.33, bf16[128,512]{1,0:T(8,128)(2,1)S(1)} %bitcast.34), custom_call_target="tpu_custom_call" | custom-call | flops 10000000000 | bytes 8000000 | tf_op jit(solution)/shard_map/pallas_call | solution.py:268
  169.0 0.0 copy-start.5
  169.1 1.0 copy-done.5
  170.0 0.0 collective-permute-done
  170.0 0.0 copy-done.7
  170.0 0.2 maximum_select_fusion.x_ref
  170.3 0.0 all-gather.2.cloned.1.call-done.w_ref
  170.3 0.0 copy-start.6
  170.3 1.2 copy-done.6
  171.5 15.9 %shard_map.112 = (bf16[2,128,2560]{2,1,0:T(8,128)(2,1)S(1)}, bf16[160,128,128]{2,1,0:T(8,128)(2,1)}) custom-call(s32[320]{0:T(512)S(1)} %reshape.18.inv_ref, s32[160]{0:T(256)S(1)} %reshape.19.rows_ref, bf16[2,128,2048]{2,1,0:T(8,128)(2,1)S(1)} %copy-done.6, bf16[2,128,2560]{2,1,0:T(8,128)(2,1)S(1)} %maximum_select_fusion.x_ref, ...), custom_call_target="tpu_custom_call" | custom-call | flops 4000000000 | bytes 15000000 | tf_op jit(solution)/shard_map/pallas_call | solution.py:343
  187.4 5.9 %copy.19 = bf16[160,128,128]{2,0,1:T(8,128)(2,1)S(1)} copy(bf16[160,128,128]{2,1,0:T(8,128)(2,1)} %get-tuple-element.13) | data formatting | bytes 10485760
  193.3 4.5 %copy.25 = bf16[16,8,160,128]{3,1,2,0:T(8,128)(2,1)} copy(bf16[16,8,160,128]{3,2,1,0:T(8,128)(2,1)S(1)} %bitcast.36) | data formatting | bytes 10485760
  197.7 0.0 reduce-scatter.7.cloned.1.call-update
  197.8 0.0 reduce-scatter.5.cloned.1.call-start
  197.8 0.1 dynamic-slice_bitcast_fusion
  197.9 0.1 collective-permute-start.1
  198.6 87.1 %reduce-scatter.7.cloned.1.call-done = bf16[8,20480]{1,0:T(8,128)(2,1)} async-done(((bf16[128,20480]{1,0:T(8,128)(2,1)}), bf16[8,20480]{1,0:T(8,128)(2,1)}) %reduce-scatter.7.cloned.1.call-update) | async-done | bytes 327696
  285.7 1.0 copy.26
  286.8 0.9 copy.20
  287.6 0.0 reduce-scatter.5.cloned.1.call-update
  287.6 0.0 collective-permute-done.1
  287.6 1.0 fusion.1
  288.6 36.3 %reduce-scatter.5.cloned.1.call-done = bf16[20,8,128]{2,1,0:T(8,128)(2,1)} async-done(((bf16[160,8,128]{2,1,0:T(8,128)(2,1)}), bf16[20,8,128]{2,1,0:T(8,128)(2,1)}) %reduce-scatter.5.cloned.1.call-update) | async-done | bytes 40976 | tf_op jit(solution)/shard_map/reduce_scatter | solution.py:380
  324.9 1.4 convert_divide_fusion
  326.3 0.7 copy.30
  327.0 0.7 copy.31
Async XLA Ops:
  7.2 29.6 %copy-start = (s32[32,10]{0,1:T(8,128)S(1)}, s32[32,10]{0,1:T(8,128)}, u32[]{:S(2)}) copy-start(s32[32,10]{0,1:T(8,128)} %param.14) | copy-start | bytes 3844
  7.2 30.1 %copy-start.1 = (bf16[1,128,4096]{2,1,0:T(8,128)(2,1)S(1)}, bf16[1,128,4096]{2,1,0:T(8,128)(2,1)}, u32[]{:S(2)}) copy-start(bf16[1,128,4096]{2,1,0:T(8,128)(2,1)} %param.9) | copy-start | bytes 3145732
  7.2 30.1 %copy-start.3 = (bf16[1,128,512]{2,1,0:T(8,128)(2,1)S(1)}, bf16[1,128,512]{2,1,0:T(8,128)(2,1)}, u32[]{:S(2)}) copy-start(bf16[1,128,512]{2,1,0:T(8,128)(2,1)} %param.10) | copy-start | bytes 393220
  7.2 30.1 %copy-start.4 = (bf16[1,128,512]{2,1,0:T(8,128)(2,1)S(1)}, bf16[1,128,512]{2,1,0:T(8,128)(2,1)}, u32[]{:S(2)}) copy-start(bf16[1,128,512]{2,1,0:T(8,128)(2,1)} %param.11) | copy-start | bytes 393220
  7.2 163.1 %all-gather.2.cloned.1.call-start = ((), (), s32[]{:S(2)}) async-start(), calls=%async_computation.2 | async-start | bytes 5898240 | tf_op jit(solution)/shard_map/all_gather | solution.py:366
  35.2 250.5 %reduce-scatter.7.cloned.1.call-start = ((), (), s32[]{:S(2)}) async-start(), calls=%async_computation.4 | async-start | bytes 5570560
  35.2 134.8 %collective-permute-start = (bf16[128,2560]{1,0:T(8,128)(2,1)}, bf16[128,2560]{1,0:T(8,128)(2,1)S(1)}, u32[]{:S(2)}, u32[]{:S(2)}) collective-permute-start(bf16[128,2560]{1,0:T(8,128)(2,1)} %bitcast.38), channel_id=1, source_target_pairs={{0,8},{1,9},{2,10},{3,11},{4,12},{5,13},{6,14},{7,15},{8,0},{9,1},... | collective-permute-start | bytes 1966088 | tf_op jit(solution)/shard_map/ppermute | solution.py:367
  37.3 1.2 copy-start.2
  38.5 131.5 %copy-start.7 = (bf16[1,128,2560]{2,1,0:T(8,128)(2,1)S(1)}, bf16[1,128,2560]{2,1,0:T(8,128)(2,1)}, u32[]{:S(2)}) copy-start(bf16[1,128,2560]{2,1,0:T(8,128)(2,1)} %param.8) | copy-start | bytes 1966084
  169.0 1.0 copy-start.5
  170.3 1.2 copy-start.6
  197.8 127.1 %reduce-scatter.5.cloned.1.call-start = ((), (), s32[]{:S(2)}) async-start(), calls=%async_computation.3 | async-start | bytes 368640 | tf_op jit(solution)/shard_map/reduce_scatter | solution.py:380
  197.9 89.7 %collective-permute-start.1 = (bf16[128,2560]{1,0:T(8,128)(2,1)S(1)}, bf16[128,2560]{1,0:T(8,128)(2,1)S(1)}, u32[]{:S(2)}, u32[]{:S(2)}) collective-permute-start(bf16[128,2560]{1,0:T(8,128)(2,1)S(1)} %dynamic-slice_bitcast_fusion), channel_id=1, source_target_pairs={{0,8},{1,9},{2,10},{3,11},{4,12},{5,13},{6,14},{7,15},{8,0},{9,1},... | collective-permute-start | bytes 1966088 | tf_op jit(solution)/shard_map/ppermute | solution.py:377
Sparse Core Ops, SparseCore 0:
  35.3 83.3 all-gather.1
  197.9 87.7 reduce-scatter.6
  288.2 36.5 reduce-scatter.4

commit v2 on v1

v2 whole, which is shorter than its diff:
```python
import functools

import jax
import jax.numpy as jnp
from jax import lax
from jax.experimental import pallas as pl
from jax.experimental.pallas import tpu as pltpu
from jax.sharding import PartitionSpec as P

D = 2560
W = 128
KEEP = 10
RTILES = 20
ZN = 8
HALF = 2048
HP = 4
R = HP * W
CK = 512
KB = CK // W
YN = 4
TZ = 20
SCALE = W**-0.5
VMEM_LIMIT = 60 * 2**20
EXP_SCALE = SCALE * 1.4426950408889634
MESH = pl.DeviceIdType.MESH
F32 = jnp.float32
BF16 = jnp.bfloat16


def dot_t(a, b):
    return lax.dot_general(a, b, (((1,), (1,)), ((), ())), preferred_element_type=F32)


def dot(a, b):
    return lax.dot_general(a, b, (((1,), (0,)), ((), ())), preferred_element_type=F32)


def fold(x, op):
    return op(x.reshape(x.shape[0] // 8, 8, x.shape[1]), axis=0)


def attend(g, blk, head, z, qbuf, dobuf, kv, kt, acc, e_scr, dp_scr, q_s, do_s, dq_t, dq_ref):
    for i in range(HP):
        cols = pl.ds(pl.multiple_of((head + i) * W, W), W)
        q_s[i * W : (i + 1) * W, :] = qbuf[blk, :, cols]
        do_s[i * W : (i + 1) * W, :] = dobuf[blk, :, cols]
    t = blk * ZN + z
    full = t // KB

    def chunk(ref, c):
        return kv[ref, g, c // (ZN // KB), pl.ds((c % (ZN // KB)) * KB, KB)].reshape(CK, W)

    def rows(c):
        return pl.ds(pl.multiple_of(c * CK, CK), CK)

    def scores(c, top):
        s = dot_t(chunk(0, c), q_s[...])
        e_scr[rows(c), :] = s
        return jnp.maximum(top, fold(s, jnp.max))

    top = lax.fori_loop(0, full, scores, jnp.full((8, R), -1e30, F32))
    s = dot_t(chunk(0, full), q_s[...])
    key = full * CK + lax.broadcasted_iota(jnp.int32, (CK, R), 0)
    pos = t * W + lax.broadcasted_iota(jnp.int32, (CK, R), 1) % W
    s = jnp.where(key <= pos, s, -1e30)
    e_scr[rows(full), :] = s
    top = jnp.max(jnp.maximum(top, fold(s, jnp.max)), axis=0, keepdims=True)

    def exps(c, carry):
        total, weighted = carry
        e = jnp.exp2((e_scr[rows(c), :] - top) * EXP_SCALE)
        dp = dot_t(chunk(1, c), do_s[...])
        e_scr[rows(c), :] = e
        dp_scr[rows(c), :] = dp
        return total + fold(e, jnp.sum), weighted + fold(e * dp, jnp.sum)

    zero = jnp.zeros((8, R), F32)
    total, weighted = lax.fori_loop(0, full + 1, exps, (zero, zero))
    inv = 1.0 / jnp.sum(total, axis=0, keepdims=True)
    delta = jnp.sum(weighted, axis=0, keepdims=True) * inv
    dq_t[...] = jnp.zeros_like(dq_t)

    def grads(c, carry):
        p = e_scr[rows(c), :] * inv
        ds = (p * (dp_scr[rows(c), :] - delta)).astype(BF16)
        acc[0, g, rows(c), :] += dot(ds, q_s[...])
        acc[1, g, rows(c), :] += dot(p.astype(BF16), do_s[...])
        dq_t[...] += dot(kt[g, :, pl.ds(pl.multiple_of(c * CK, CK), CK)], ds)
        return carry

    lax.fori_loop(0, full + 1, grads, 0)
    for i in range(HP):
        cols = pl.ds(pl.multiple_of((head + i) * W, W), W)
        dq_ref[blk, :, cols] = (dq_t[:, i * W : (i + 1) * W] * SCALE).T.astype(BF16)


def fused_kernel(
    inv_ref, rows_ref, x_ref, q_ref, k_ref, v_ref, do_ref, w_ref,
    dx_ref, dk_ref, dv_ref, dw_ref,
    qbuf, dobuf, kv, kt, acc, e_scr, dp_scr, q_s, do_s, dq_t, dq,
    xbuf, xt, wg, wt, wcat, dws, core_in, y_in, s2, z_in, xh_out, xh_in,
    dx_own, dx_out, dx_in, out_r, in_r, out_l, in_l, swap_out, swap_in,
    own_sem, kv_send, kv_recv, q_send, q_recv, x_send, x_recv,
    ring_send, ring_recv, wx_send, wx_recv, wz_send, wz_recv, wy_send, wy_recv, wc_send, wc_recv,
    rs_send, rs_recv, swap_send, swap_recv, c_send, c_recv, y_send, y_recv, z_send, z_recv,
    xh_send, xh_recv, dx_send, dx_recv,
):
    s = lax.axis_index("seq")
    dp = lax.axis_index("dp")
    h, z = s // ZN, s % ZN
    y, xh, core = dp // 4, (dp // 2) % 2, dp % 2
    partner = {"seq": (1 - h) * ZN + z}
    right = {"seq": h * ZN + (z + 1) % ZN}
    left = {"seq": h * ZN + (z + ZN - 1) % ZN}
    y_peer = [{"dp": (y + j) % YN * 4 + xh * 2 + core} for j in range(1, YN)]
    xh_peer = {"dp": y * 4 + (1 - xh) * 2 + core}
    core_peer = {"dp": y * 4 + xh * 2 + 1 - core}
    z_peer = [{"seq": h * ZN + (z + j) % ZN} for j in range(1, ZN)]
    barrier = pltpu.get_barrier_semaphore()
    peers = [partner, xh_peer, core_peer] + y_peer + z_peer
    for d in peers:
        pl.semaphore_signal(barrier, inc=1, device_id=d, device_id_type=MESH)

    def remote(src, dst, ssem, rsem, d):
        return pltpu.make_async_remote_copy(src, dst, ssem, rsem, device_id=d, device_id_type=MESH)

    def cols(start, size):
        return pl.ds(pl.multiple_of(start, W), size)

    own = []

    def local(src, dst):
        c = pltpu.make_async_copy(src, dst, own_sem.at[len(own)])
        c.start()
        own.append(c)

    for g in range(2):
        for i, src in enumerate((k_ref, v_ref)):
            local(src.at[:, cols((h * 2 + g) * W, W)], kv.at[i, g, h, z])
    local(w_ref, wg.at[core, y, z, xh])
    local(x_ref, xbuf.at[h])
    for g in range(2):
        for src, buf in ((q_ref, qbuf), (do_ref, dobuf)):
            local(src.at[:, cols(h * HALF + g * 1024, 1024)], buf.at[h, :, pl.ds(g * 1024, 1024)])
    pl.semaphore_wait(barrier, len(peers))

    swaps = []
    for g in range(2):
        swaps.append([remote(src.at[:, cols(((1 - h) * 2 + g) * W, W)], kv.at[i, g, h, z],
                             kv_send.at[g, i], kv_recv.at[g, i], partner) for i, src in enumerate((k_ref, v_ref))])
    q_copies = []
    for g in range(2):
        q_copies.append([remote(src.at[:, cols((1 - h) * HALF + g * 1024, 1024)], buf.at[h, :, pl.ds(g * 1024, 1024)],
                                q_send.at[g, i], q_recv.at[g, i], partner)
                         for i, (src, buf) in enumerate(((q_ref, qbuf), (do_ref, dobuf)))])
    x_copy = remote(x_ref, xbuf.at[h], x_send, x_recv, partner)
    wx = remote(w_ref, wg.at[core, y, z, xh], wx_send, wx_recv, xh_peer)
    for c in swaps[0] + [wx] + swaps[1] + q_copies[0] + [x_copy] + q_copies[1]:
        c.start()

    def ring_at(way, step):
        return ((z + ZN - step) % ZN, right) if way == 0 else ((z + step) % ZN, left)

    def ring(g, way, step):
        at, to = ring_at(way, step)
        ref = kv.at[way, g, :, at] if step == 3 else kv.at[:, g, :, at]
        return remote(ref, ref, ring_send.at[g, way, step], ring_recv.at[g, way, step], to)

    def wring(way, step):
        at, to = ring_at(way, step)
        ref = wg.at[core, y, at, way] if step == 3 else wg.at[core, y, at]
        return remote(ref, ref, wz_send.at[way, step], wz_recv.at[way, step], to)

    def to_y(at, j):
        ref = wg.at[core, y, at]
        return remote(ref, ref, wy_send.at[at, j], wy_recv.at[at, j], y_peer[j])

    def ring_start(g):
        for i in range(2):
            swaps[g][i].wait_recv()
        for way in range(2):
            ring(g, way, 0).start()

    def ring_step(g, step):
        for way in range(2):
            ring(g, way, step).wait_recv()
            if step < 3:
                ring(g, way, step + 1).start()

    def w_start():
        wx.wait_recv()
        for way in range(2):
            wring(way, 0).start()
        for j in range(3):
            to_y(z, j).start()

    def w_step(step):
        for way in range(2):
            wring(way, step).wait_recv()
            if step < 3:
                wring(way, step + 1).start()
                for j in range(3):
                    to_y((z + ZN - 1 - step) % ZN if way == 0 else (z + 1 + step) % ZN, j).start()
        if step == 3:
            for j in range(3):
                to_y((z + 4) % ZN, j).start()

    w_core = remote(wg.at[core], wg.at[core], wc_send, wc_recv, core_peer)

    def w_swap():
        def one(i, carry):
            for j in range(3):
                to_y(i, j).wait_recv()
            return carry

        lax.fori_loop(0, ZN, one, 0)
        w_core.start()

    def turn_keys(g):
        def one(b, carry):
            kt[g, :, cols(b * W, W)] = kv[0, g, b // ZN, b % ZN].T
            return carry

        lax.fori_loop(0, 2 * ZN, one, 0)

    def turn_x(blk):
        def one(r, carry):
            xt[r, blk] = xbuf[blk, :, cols(r * W, W)].T
            return carry

        lax.fori_loop(0, RTILES, one, 0)

    acc[...] = jnp.zeros_like(acc)
    for c in own[:4]:
        c.wait()
    ring_start(0)
    own[4].wait()
    own[5].wait()
    turn_x(h)
    for step in range(4):
        ring_step(0, step)
    ring_start(1)
    turn_keys(0)
    for c in own[6:]:
        c.wait()

    def package(g, d):
        return [[acc[i, g, cols((hl * ZN + d) * W, W), :] * (SCALE if i == 0 else 1.0)
                 for hl in range(2)] for i in range(2)]

    def rs(g, way, step):
        src, dst, to = ((out_r, in_r, right), (out_l, in_l, left))[way]
        return remote(src.at[g, step], dst.at[g, step], rs_send.at[g, way, step], rs_recv.at[g, way, step], to)

    def rs_step(g, step):
        for way, n in ((0, 4), (1, 3)):
            if step >= n:
                continue
            src, dst = ((out_r, in_r), (out_l, in_l))[way]
            d = (z + 4 - step) % ZN if way == 0 else (z + ZN - 3 + step) % ZN
            part = package(g, d)
            if step > 0:
                rs(g, way, step - 1).wait_recv()
            for i in range(2):
                for hl in range(2):
                    v = part[i][hl]
                    if step > 0:
                        v = v + dst[g, step - 1, i, hl].astype(F32)
                    src[g, step, i, hl] = v.astype(BF16)
            rs(g, way, step).start()

    def pair(g):
        return remote(swap_out.at[g], swap_in.at[g], swap_send.at[g], swap_recv.at[g], partner)

    def rs_end(g):
        part = package(g, z)
        rs(g, 0, 3).wait_recv()
        rs(g, 1, 2).wait_recv()
        for i, out in enumerate((dk_ref, dv_ref)):
            both = [part[i][hl] + in_r[g, 3, i, hl].astype(F32) + in_l[g, 2, i, hl].astype(F32) for hl in range(2)]
            mine = jnp.where(h == 0, both[0], both[1])
            other = jnp.where(h == 0, both[1], both[0])
            out[:, cols((h * 2 + g) * W, W)] = mine.astype(BF16)
            swap_out[g, i] = other.astype(BF16)
        pair(g).start()

    def rs_out(g):
        pair(g).wait_recv()
        for i, out in enumerate((dk_ref, dv_ref)):
            out[:, cols(((1 - h) * 2 + g) * W, W)] = swap_in[g, i]

    def dw_tiles(p):
        for c4 in range(4):
            c = p * 4 + c4
            xs = jnp.concatenate(
                [jnp.concatenate([xt[rows_ref[c * KEEP + k], b] for b in range(2)], axis=1) for k in range(KEEP)], axis=0)
            out = dot(xs, dq[:, :, cols(c * W, W)].reshape(2 * W, W))
            out = out.reshape(KEEP, YN, 2, 2, 8, W)
            for cc in range(2):
                for yy in range(YN):
                    dws[p, cc, yy, c4 // 2, pl.ds((c4 % 2) * KEEP, KEEP)] = (
                        out[:, yy, :, cc].reshape(KEEP, 16, W).astype(BF16))
        to_core(p).start()

    def to_core(p):
        return remote(dws.at[p, 1 - core], core_in.at[p], c_send.at[p], c_recv.at[p], core_peer)

    def dw_y(p, j):
        return remote(dws.at[p, core, (y + j + 1) % YN], y_in.at[p, j], y_send.at[p, j], y_recv.at[p, j], y_peer[j])

    def dw_to_y(p):
        to_core(p).wait_recv()
        for j in (1, 0, 2):
            yy = (y + j + 1) % YN
            dws[p, core, yy] = (dws[p, core, yy].astype(F32) + core_in[p, yy].astype(F32)).astype(BF16)
            dw_y(p, j).start()
        dws[p, core, y] = (dws[p, core, y].astype(F32) + core_in[p, y].astype(F32)).astype(BF16)

    def dw_z(p, i):
        return remote(s2.at[p, i], z_in.at[z], z_send.at[p, i], z_recv.at[z], {"seq": h * ZN + p * 2 + i})

    def dw_to_z(p):
        for j in range(3):
            dw_y(p, j).wait_recv()
        for i in range(2):
            v = dws[p, core, y, i].astype(F32)
            for j in range(3):
                v = v + y_in[p, j, i].astype(F32)
            s2[p, i] = v.astype(BF16)

            @pl.when(p * 2 + i != z)
            def _():
                dw_z(p, i).start()

    xh_copy = remote(xh_out, xh_in, xh_send, xh_recv, xh_peer)

    def dw_to_x():
        z_in[z] = s2[z // 2, z % 2]
        for i in range(ZN):

            @pl.when(i != z)
            def _():
                remote(z_in.at[i], z_in.at[i], z_send.at[0, 0], z_recv.at[i], partner).wait_recv()

        total = z_in[0].astype(F32)
        for i in range(1, ZN):
            total = total + z_in[i].astype(F32)
        low, high = total[:, :8], total[:, 8:]
        dw_ref[...] = jnp.where(xh == 0, low, high)
        xh_out[...] = jnp.where(xh == 0, high, low)
        xh_copy.start()

    def dw_end():
        xh_copy.wait_recv()
        dw_ref[...] += xh_in[...]

    def when(cond, f):
        pl.when(cond)(f)

    def work(it, carry):
        g = it // 4
        blk = jnp.where(it % 2 == 0, h, 1 - h)
        head = it // 2 * HP
        for i in range(4):
            when(it == i, functools.partial(ring_step, 1, i))
            when(it == 4 + i, functools.partial(rs_step, 0, i))
            when(it == 1 + i, functools.partial(w_step, i))
        when(it == 0, w_start)
        when(it == 7, w_swap)
        for gg in range(2):

            @pl.when(it == gg * 4 + 1)
            def _():
                for c in q_copies[gg]:
                    c.wait_recv()

        @pl.when(it == 2)
        def _():
            x_copy.wait_recv()
            turn_x(1 - h)

        when(it == 4, functools.partial(turn_keys, 1))

        @pl.when((it % 2 == 0) & (it > 1))
        def _():
            dw_tiles(it // 2 - 1)

        @pl.when((it % 2 == 1) & (it > 2))
        def _():
            dw_to_y(it // 2 - 1)

        @pl.when((it % 2 == 1) & (it > 4))
        def _():
            dw_to_z(it // 2 - 2)

        attend(g, blk, head, z, qbuf, dobuf, kv, kt, acc, e_scr, dp_scr, q_s, do_s, dq_t, dq)
        return carry

    lax.fori_loop(0, 8, work, 0)

    def assemble(i, carry):
        zz, m = i // (TZ // 2), i % (TZ // 2)
        v = wg[:, :, zz, :, pl.ds(pl.multiple_of(m * 16, 16), 16), :].astype(F32).reshape(2, YN, 2, 2, 8, W)
        v = v.transpose(3, 1, 2, 0, 4, 5).reshape(2, W, W)
        wt[pl.ds(zz * TZ + m * 2, 2)] = v.astype(BF16)
        return carry

    def dx_part(r2):
        part = cols(r2 * 2 * W, 2 * W)
        return remote(dx_out.at[:, part], dx_in.at[:, part], dx_send.at[r2], dx_recv.at[r2], partner)

    def dx_step(r2, carry):
        for i in range(2):
            for c in range(16):
                k = inv_ref[(r2 * 2 + i) * 16 + c]
                tile = wt[c * KEEP + jnp.minimum(k, KEEP - 1)]
                wcat[i * W : (i + 1) * W, c * W : (c + 1) * W] = jnp.where(k < KEEP, tile, jnp.zeros_like(tile))
        part = cols(r2 * 2 * W, 2 * W)
        out = dot_t(dq[...].reshape(2 * W, HALF), wcat[...])
        first, second = out[:W], out[W:]
        dx_out[:, part] = jnp.where(h == 0, second, first).astype(BF16)
        dx_part(r2).start()
        dx_own[:, part] = jnp.where(h == 0, first, second)
        return carry

    def dx_end(r2, carry):
        dx_part(r2).wait_recv()
        part = cols(r2 * 2 * W, 2 * W)
        dx_ref[:, part] = (dx_own[:, part] + dx_in[:, part].astype(F32)).astype(BF16)
        return carry

    dw_tiles(3)
    rs_step(1, 0)
    rs_end(0)
    dw_to_z(2)
    dw_to_y(3)
    rs_step(1, 1)
    w_core.wait_recv()
    lax.fori_loop(0, ZN * TZ // 2, assemble, 0)
    rs_step(1, 2)
    lax.fori_loop(0, 4, dx_step, 0)
    rs_step(1, 3)
    dw_to_z(3)
    lax.fori_loop(4, 10, dx_step, 0)
    rs_end(1)
    dw_to_x()
    rs_out(0)
    rs_out(1)
    lax.fori_loop(0, 10, dx_end, 0)
    dw_end()

    for c in swaps[0] + swaps[1] + q_copies[0] + q_copies[1] + [x_copy, wx, w_core, xh_copy]:
        c.wait_send()
    for way in range(2):
        for step in range(4):
            ring(0, way, step).wait_send()
            ring(1, way, step).wait_send()
            wring(way, step).wait_send()
    for g in range(2):
        for way, n in ((0, 4), (1, 3)):
            for step in range(n):
                rs(g, way, step).wait_send()
        pair(g).wait_send()

    def sent_w(i, carry):
        for j in range(3):
            to_y(i, j).wait_send()
        return carry

    lax.fori_loop(0, ZN, sent_w, 0)

    def sent_dw(p, carry):
        to_core(p).wait_send()
        for j in range(3):
            dw_y(p, j).wait_send()
        for i in range(2):

            @pl.when(p * 2 + i != z)
            def _():
                dw_z(p, i).wait_send()

        return carry

    lax.fori_loop(0, 4, sent_dw, 0)

    def sent_dx(r2, carry):
        dx_part(r2).wait_send()
        return carry

    lax.fori_loop(0, 10, sent_dx, 0)


def fused(inv, rows, x, q, k, v, do, w):
    any_spec = pl.BlockSpec(memory_space=pl.ANY)
    vmem = pl.BlockSpec(memory_space=pltpu.VMEM)
    smem = pl.BlockSpec(memory_space=pltpu.SMEM)
    dma = pltpu.SemaphoreType.DMA

    def low(*shape):
        return pltpu.VMEM(shape, BF16)

    def full(*shape):
        return pltpu.VMEM(shape, F32)

    return pl.pallas_call(
        fused_kernel,
        out_shape=(
            jax.ShapeDtypeStruct((W, D), BF16),
            jax.ShapeDtypeStruct((W, 512), BF16),
            jax.ShapeDtypeStruct((W, 512), BF16),
            jax.ShapeDtypeStruct((TZ, 8, W), F32),
        ),
        in_specs=[smem] * 2 + [any_spec] * 6,
        out_specs=(vmem,) * 4,
        scratch_shapes=[
            low(2, W, HALF), low(2, W, HALF), low(2, 2, 2, ZN, W, W), low(2, W, 2048), full(2, 2, 2048, W),
            full(2048, R), full(2048, R), low(R, W), low(R, W), full(W, R), low(2, W, HALF),
            low(2, W, D), low(RTILES, 2, W, W), low(2, YN, ZN, 2, TZ * 8, W), low(ZN * TZ, W, W), low(2 * W, HALF),
            low(4, 2, YN, 2, TZ, 16, W), low(4, YN, 2, TZ, 16, W), low(4, 3, 2, TZ, 16, W), low(4, 2, TZ, 16, W),
            low(ZN, TZ, 16, W), full(TZ, 8, W), full(TZ, 8, W),
            full(W, D), low(W, D), low(W, D),
            low(2, 4, 2, 2, W, W), low(2, 4, 2, 2, W, W), low(2, 3, 2, 2, W, W), low(2, 3, 2, 2, W, W),
            low(2, 2, W, W), low(2, 2, W, W),
            dma((10,)), dma((2, 2)), dma((2, 2)), dma((2, 2)), dma((2, 2)), dma, dma,
            dma((2, 2, 4)), dma((2, 2, 4)), dma, dma, dma((2, 4)), dma((2, 4)), dma((ZN, 3)), dma((ZN, 3)), dma, dma,
            dma((2, 2, 4)), dma((2, 2, 4)), dma((2,)), dma((2,)), dma((4,)), dma((4,)), dma((4, 3)), dma((4, 3)),
            dma((4, 2)), dma((ZN,)), dma, dma, dma((10,)), dma((10,)),
        ],
        compiler_params=pltpu.CompilerParams(
            collective_id=0, has_side_effects=True, vmem_limit_bytes=VMEM_LIMIT
        ),
        cost_estimate=pl.CostEstimate(flops=14 * 10**9, bytes_accessed=8 * 10**6, transcendentals=10**7),
    )(inv, rows, x, q, k, v, do, w)


def body(x, q, k, v, do, w, tile_rows, loss_scale):
    h = lax.axis_index("seq") // ZN
    my_rows = lax.dynamic_slice_in_dim(tile_rows, h * 16, 16, 0)
    hit = my_rows[:, :, None] == jnp.arange(RTILES, dtype=jnp.int32)
    inv = jnp.min(jnp.where(hit, jnp.arange(KEEP, dtype=jnp.int32)[None, :, None], KEEP), axis=1).T.reshape(-1)
    dx, dk, dv, dw = fused(
        inv, my_rows.reshape(-1), x[0], q[0], k[0], v[0], do[0], w.reshape(TZ * 8, W))
    return dx[None], dk[None], dv[None], dw / loss_scale[0].astype(F32)


def solution(mesh):
    tokens = P("dp", "seq", None)
    tiles = P("seq", "dp", None)
    return jax.shard_map(
        body,
        mesh=mesh,
        in_specs=(tokens,) * 5 + (tiles, P(), P()),
        out_specs=(tokens, tokens, tokens, tiles),
        check_vma=False,
    )
```

time: 335 us -> 137 us (0.41)
  the two profiles are of different devices: /device:TPU:2 before, /device:TPU:248 now
where the time goes in v2:
time: 137 us
  Pallas kernels  128 us (93%)
  local copies, waits for them, and re-layouts  5.84 us (4%)
  other arithmetic  1.63 us (1%)
    pallas_call x1, Pallas kernels, fused(): pl.pallas_call(fused_kernel, out_shape=(jax.ShapeDtypeStruct((W, D), BF16...  128 us
    unnamed x9, local copies, waits for them, and re-layouts  4.29 us

profile of v2, /device:TPU:248, one launch (start us, length us, event | category | flops | bytes accessed | tf_op | source)
XLA Modules:
  0.0 137.0 jit_solution(13832531823837562216)
XLA Ops:
  0.6 0.0 copy-start
  0.7 0.7 copy-done
  1.3 0.1 constant_dynamic-slice_fusion
  1.4 0.1 select_reduce_fusion
  1.5 0.1 copy.15
  1.6 0.7 reshape.19.inv_ref
  2.3 0.1 copy.16
  2.3 0.7 reshape.20.rows_ref
  3.0 128.3 %shard_map.111 = (bf16[128,2560]{1,0:T(8,128)(2,1)}, bf16[128,512]{1,0:T(8,128)(2,1)}, bf16[128,512]{1,0:T(8,128)(2,1)}, f32[20,8,128]{2,1,0:T(8,128)}) custom-call(s32[320]{0:T(512)} %reshape.19.inv_ref, s32[160]{0:T(256)} %reshape.20.rows_ref, bf16[128,2560]{1,0:T(8,128)(2,1)} %bitcast.17, bf16[128,4096]{1,0:T(8,128)(2,1)} %bitcast.15, ...), custom_call_target="tpu_custom_call" | custom-call | flops 14000000000 | bytes 8000000 | tf_op jit(solution)/shard_map/pallas_call | solution.py:505
  131.9 1.5 %broadcast_divide_fusion = f32[20,8,128]{2,1,0:T(8,128)} fusion(f32[20,8,128]{2,1,0:T(8,128)} %get-tuple-element.11, f32[]{:T(128)} %bitcast.10), kind=kLoop, calls=%fused_computation.2 | loop fusion | flops 20480 | bytes 163844 | tf_op jit(solution)/shard_map/div | solution.py:543
  133.4 0.0 copy-start.2
  133.4 2.0 %copy.21 = bf16[1,128,2560]{2,1,0:T(8,128)(2,1)} copy(bf16[1,128,2560]{2,1,0:T(8,128)(2,1)} %bitcast.11) | data formatting | bytes 1310720
  135.4 0.0 copy-done.2
  135.4 0.0 copy-start.1
  135.4 0.7 copy.22
  136.1 0.3 copy-done.1
  136.4 0.7 copy.23
Async XLA Ops:
  0.6 0.7 copy-start
  133.4 2.0 %copy-start.2 = (bf16[128,512]{1,0:T(8,128)(2,1)S(1)}, bf16[128,512]{1,0:T(8,128)(2,1)}, u32[]{:S(2)}) copy-start(bf16[128,512]{1,0:T(8,128)(2,1)} %get-tuple-element.9) | copy-start | bytes 393220
  135.4 1.0 copy-start.1

commit v3 on v2

v3 whole, which is shorter than its diff:
```python
import functools

import jax
import jax.numpy as jnp
from jax import lax
from jax.experimental import pallas as pl
from jax.experimental.pallas import tpu as pltpu
from jax.sharding import PartitionSpec as P

D = 2560
W = 128
KEEP = 10
RTILES = 20
ZN = 8
HALF = 2048
HP = 4
R = HP * W
CK = 512
KB = CK // W
YN = 4
HOPS = ((4, 3), (3, 4))
TZ = 20
SCALE = W**-0.5
VMEM_LIMIT = 60 * 2**20
EXP_SCALE = SCALE * 1.4426950408889634
MESH = pl.DeviceIdType.MESH
F32 = jnp.float32
BF16 = jnp.bfloat16


def dot_t(a, b):
    return lax.dot_general(a, b, (((1,), (1,)), ((), ())), preferred_element_type=F32)


def dot(a, b):
    return lax.dot_general(a, b, (((1,), (0,)), ((), ())), preferred_element_type=F32)


def fold(x, op):
    return op(x.reshape(x.shape[0] // 8, 8, x.shape[1]), axis=0)


def attend(g, blk, head, z, qbuf, dobuf, kv, kt, acc, e_scr, dp_scr, q_s, do_s, dq_t, dq_ref, tick):
    tick(0)
    for i in range(HP):
        cols = pl.ds(pl.multiple_of((head + i) * W, W), W)
        q_s[i * W : (i + 1) * W, :] = qbuf[blk, :, cols]
        do_s[i * W : (i + 1) * W, :] = dobuf[blk, :, cols]
    t = blk * ZN + z
    full = t // KB

    def chunk(ref, c):
        return kv[ref, g, c // (ZN // KB), pl.ds((c % (ZN // KB)) * KB, KB)].reshape(CK, W)

    def rows(c):
        return pl.ds(pl.multiple_of(c * CK, CK), CK)

    def scores(c, top):
        s = dot_t(chunk(0, c), q_s[...])
        e_scr[rows(c), :] = s
        return jnp.maximum(top, fold(s, jnp.max))

    top = lax.fori_loop(0, full, scores, jnp.full((8, R), -1e30, F32))
    s = dot_t(chunk(0, full), q_s[...])
    key = full * CK + lax.broadcasted_iota(jnp.int32, (CK, R), 0)
    pos = t * W + lax.broadcasted_iota(jnp.int32, (CK, R), 1) % W
    s = jnp.where(key <= pos, s, -1e30)
    e_scr[rows(full), :] = s
    top = jnp.max(jnp.maximum(top, fold(s, jnp.max)), axis=0, keepdims=True)

    tick(1)

    def exps(c, carry):
        total, weighted = carry
        e = jnp.exp2((e_scr[rows(c), :] - top) * EXP_SCALE)
        dp = dot_t(chunk(1, c), do_s[...])
        e_scr[rows(c), :] = e
        dp_scr[rows(c), :] = dp
        return total + fold(e, jnp.sum), weighted + fold(e * dp, jnp.sum)

    zero = jnp.zeros((8, R), F32)
    total, weighted = lax.fori_loop(0, full + 1, exps, (zero, zero))
    inv = 1.0 / jnp.sum(total, axis=0, keepdims=True)
    delta = jnp.sum(weighted, axis=0, keepdims=True) * inv
    dq_t[...] = jnp.zeros_like(dq_t)
    tick(2)

    def grads(c, carry):
        p = e_scr[rows(c), :] * inv
        ds = (p * (dp_scr[rows(c), :] - delta)).astype(BF16)
        acc[0, g, rows(c), :] += dot(ds, q_s[...])
        acc[1, g, rows(c), :] += dot(p.astype(BF16), do_s[...])
        dq_t[...] += dot(kt[g, :, pl.ds(pl.multiple_of(c * CK, CK), CK)], ds)
        return carry

    lax.fori_loop(0, full + 1, grads, 0)
    for i in range(HP):
        cols = pl.ds(pl.multiple_of((head + i) * W, W), W)
        dq_ref[blk, :, cols] = (dq_t[:, i * W : (i + 1) * W] * SCALE).T.astype(BF16)


def fused_kernel(
    rows_ref, x_ref, q_ref, k_ref, v_ref, do_ref, w_ref,
    dx_ref, dk_ref, dv_ref, dw_ref,
    qbuf, dobuf, kv, kt, acc, e_scr, dp_scr, q_s, do_s, dq_t, dq,
    xbuf, xt, wg, wt, wcat, dws, core_in, y_in, s2, z_out, z_in, xh_out, xh_in,
    at_ref, inv_ref, dx_own, dx_out, dx_in, out_r, in_r, out_l, in_l, swap_out, swap_in,
    own_sem, kv_send, kv_recv, q_send, q_recv, x_send, x_recv,
    ring_send, ring_recv, wx_send, wx_recv, wz_send, wz_recv, wy_send, wy_recv, wp_send, wp_recv, wc_send, wc_recv,
    rs_send, rs_recv, swap_send, swap_recv, c_send, c_recv, y_send, y_recv, z_send, z_recv,
    xh_send, xh_recv, dx_send, dx_recv,
):
    s = lax.axis_index("seq")
    dp = lax.axis_index("dp")
    h, z = s // ZN, s % ZN
    y, xh, core = dp // 4, (dp // 2) % 2, dp % 2
    partner = {"seq": (1 - h) * ZN + z}
    right = {"seq": h * ZN + (z + 1) % ZN}
    left = {"seq": h * ZN + (z + ZN - 1) % ZN}
    y_peer = [{"dp": (y + j) % YN * 4 + xh * 2 + core} for j in range(1, YN)]
    xh_peer = {"dp": y * 4 + (1 - xh) * 2 + core}
    core_peer = {"dp": y * 4 + xh * 2 + 1 - core}
    barrier = pltpu.get_barrier_semaphore()
    peers = [partner, xh_peer, core_peer, right, left] + y_peer
    for d in peers:
        pl.semaphore_signal(barrier, inc=1, device_id=d, device_id_type=MESH)

    def remote(src, dst, ssem, rsem, d):
        return pltpu.make_async_remote_copy(src, dst, ssem, rsem, device_id=d, device_id_type=MESH)

    def cols(start, size):
        return pl.ds(pl.multiple_of(start, W), size)

    own = []

    def local(src, dst):
        c = pltpu.make_async_copy(src, dst, own_sem.at[len(own)])
        c.start()
        own.append(c)

    for g in range(2):
        for i, src in enumerate((k_ref, v_ref)):
            local(src.at[:, cols((h * 2 + g) * W, W)], kv.at[i, g, h, z])
    local(w_ref, wg.at[core, y, z, xh])
    local(x_ref, xbuf.at[h])
    for g in range(2):
        for src, buf in ((q_ref, qbuf), (do_ref, dobuf)):
            local(src.at[:, cols(h * HALF + g * 1024, 1024)], buf.at[h, :, pl.ds(g * 1024, 1024)])
    pl.semaphore_wait(barrier, len(peers))

    swaps = []
    for g in range(2):
        swaps.append([remote(src.at[:, cols(((1 - h) * 2 + g) * W, W)], kv.at[i, g, h, z],
                             kv_send.at[g, i], kv_recv.at[g, i], partner) for i, src in enumerate((k_ref, v_ref))])
    q_copies = []
    for n in range(4):
        q_copies.append([remote(src.at[:, cols((1 - h) * HALF + n * R, R)], buf.at[h, :, pl.ds(n * R, R)],
                                q_send.at[n, i], q_recv.at[n, i], partner)
                         for i, (src, buf) in enumerate(((q_ref, qbuf), (do_ref, dobuf)))])
    x_copy = remote(x_ref, xbuf.at[h], x_send, x_recv, partner)
    wx = remote(w_ref, wg.at[core, y, z, xh], wx_send, wx_recv, xh_peer)
    for c in swaps[0] + [wx] + q_copies[0] + q_copies[1] + swaps[1] + [x_copy] + q_copies[2] + q_copies[3]:
        c.start()

    def ring_at(way, step):
        return ((z + ZN - step) % ZN, right) if way == 0 else ((z + step) % ZN, left)

    def ring(g, i, way, step):
        at, to = ring_at(way, step)
        ref = kv.at[i, g, :, at]
        return remote(ref, ref, ring_send.at[g, i, way, step], ring_recv.at[g, i, way, step], to)

    def wring(way, step):
        at, to = ring_at(way, step)
        ref = wg.at[core, y, at, way] if step == 3 else wg.at[core, y, at]
        return remote(ref, ref, wz_send.at[way, step], wz_recv.at[way, step], to)

    def to_y(at, j):
        ref = wg.at[core, y, at]
        return remote(ref, ref, wy_send.at[at, j], wy_recv.at[at, j], y_peer[2 * j])

    def y_pass(j):
        ref = wg.at[core, (y + (3, 1)[j]) % YN, :, j]
        return remote(ref, ref, wp_send.at[j], wp_recv.at[j], y_peer[2 * j])

    def ring_start(g, i):
        swaps[g][i].wait_recv()
        for way in range(2):
            ring(g, i, way, 0).start()

    def ring_step(g, i, step):
        for way in range(2):
            if step < HOPS[i][way]:
                ring(g, i, way, step).wait_recv()
                if step + 1 < HOPS[i][way]:
                    ring(g, i, way, step + 1).start()

    def w_to_y(at):
        for j in range(2):
            to_y(at, j).start()

    def w_start():
        wx.wait_recv()
        for way in range(2):
            wring(way, 0).start()
        w_to_y(z)

    def w_step(step):
        for way in range(2):
            wring(way, step).wait_recv()
            if step < 3:
                wring(way, step + 1).start()
                w_to_y((z + ZN - 1 - step) % ZN if way == 0 else (z + 1 + step) % ZN)
        if step == 3:
            w_to_y((z + 4) % ZN)

    def w_pass():
        def one(i, carry):
            for j in range(2):
                to_y(i, j).wait_recv()
            return carry

        lax.fori_loop(0, ZN, one, 0)
        for j in range(2):
            y_pass(j).start()

    w_core = remote(wg.at[core], wg.at[core], wc_send, wc_recv, core_peer)

    def w_swap():
        for j in range(2):
            y_pass(j).wait_recv()
        w_core.start()

    def turn_keys(g):
        def one(b, carry):
            kt[g, :, cols(b * W, W)] = kv[0, g, b // ZN, b % ZN].T
            return carry

        lax.fori_loop(0, 2 * ZN, one, 0)

    def turn_x(blk):
        def one(r, carry):
            xt[r, blk] = xbuf[blk, :, cols(r * W, W)].T
            return carry

        lax.fori_loop(0, RTILES, one, 0)

    for c in range(16):
        at_ref[c] = 0
    for c in own[:5]:
        c.wait()
    ring_start(0, 0)
    ring_start(0, 1)
    def find(r, carry):
        for c in range(16):
            k = at_ref[c]
            last = jnp.minimum(k, KEEP - 1)
            kept = (k < KEEP) & (rows_ref[h * 16 + c, last] == r)
            at_ref[c] = k + kept.astype(jnp.int32)
            inv_ref[r * 16 + c] = jnp.where(kept, c * KEEP + last, -1)
        return carry

    acc[...] = jnp.zeros_like(acc)
    own[5].wait()
    for step in range(4):
        ring_step(0, 0, step)
        ring_step(0, 1, step)
        if step == 1:
            turn_x(h)
        if step < 3:
            lax.fori_loop(step * 7, min(step * 7 + 7, RTILES), find, 0)
        if step == 0:
            w_start()
        else:
            w_step(step - 1)
        if step == 2:
            ring_start(1, 0)
            ring_start(1, 1)
    turn_keys(0)
    for c in own[6:]:
        c.wait()

    def piece(g, i, hl, d):
        return acc[i, g, cols((hl * ZN + d) * W, W), :] * (SCALE if i == 0 else 1.0)

    def rs(g, i, way, step):
        src, dst, to = ((out_r, in_r, right), (out_l, in_l, left))[way]
        return remote(src.at[g, step, i], dst.at[g, step, i],
                      rs_send.at[g, i, way, step], rs_recv.at[g, i, way, step], to)

    def rs_step(g, step):
        for i in range(2):
            for way in range(2):
                n = HOPS[i][way]
                if step >= n:
                    continue
                src, dst = ((out_r, in_r), (out_l, in_l))[way]
                d = (z + n - step) % ZN if way == 0 else (z + ZN - n + step) % ZN
                if step > 0:
                    rs(g, i, way, step - 1).wait_recv()
                for hl in range(2):
                    v = piece(g, i, hl, d)
                    if step > 0:
                        v = v + dst[g, step - 1, i, hl].astype(F32)
                    src[g, step, i, hl] = v.astype(BF16)
                rs(g, i, way, step).start()

    def pair(g):
        return remote(swap_out.at[g], swap_in.at[g], swap_send.at[g], swap_recv.at[g], partner)

    def rs_end(g):
        for i, out in enumerate((dk_ref, dv_ref)):
            for way in range(2):
                rs(g, i, way, HOPS[i][way] - 1).wait_recv()
            both = [piece(g, i, hl, z) + in_r[g, HOPS[i][0] - 1, i, hl].astype(F32)
                    + in_l[g, HOPS[i][1] - 1, i, hl].astype(F32) for hl in range(2)]
            out[:, cols((h * 2 + g) * W, W)] = jnp.where(h == 0, both[0], both[1]).astype(BF16)
            swap_out[g, i] = jnp.where(h == 0, both[1], both[0]).astype(BF16)
        pair(g).start()

    def rs_out(g):
        pair(g).wait_recv()
        for i, out in enumerate((dk_ref, dv_ref)):
            out[:, cols(((1 - h) * 2 + g) * W, W)] = swap_in[g, i]

    def dw_tiles(p):
        for n in range(2):
            c = p * 2 + n
            xs = jnp.concatenate(
                [jnp.concatenate([xt[rows_ref[h * 16 + c, k], b] for b in range(2)], axis=1) for k in range(KEEP)],
                axis=0)
            out = dot(xs, dq[:, :, cols(c * W, W)].reshape(2 * W, W))
            out = out.reshape(KEEP, YN, 2, 2, 8, W)
            for cc in range(2):
                for yy in range(YN):
                    dws[p, cc, yy, pl.ds(n * KEEP, KEEP)] = out[:, yy, :, cc].reshape(KEEP, 16, W).astype(BF16)
        to_core(p).start()

    def to_core(p):
        return remote(dws.at[p, 1 - core], core_in.at[p], c_send.at[p], c_recv.at[p], core_peer)

    def dw_y(p, j):
        return remote(dws.at[p, core, (y + j + 1) % YN], y_in.at[p, j], y_send.at[p, j], y_recv.at[p, j], y_peer[j])

    def dw_to_y(p):
        to_core(p).wait_recv()
        for j in (1, 0, 2):
            yy = (y + j + 1) % YN
            dws[p, core, yy] = (dws[p, core, yy].astype(F32) + core_in[p, yy].astype(F32)).astype(BF16)
            dw_y(p, j).start()
        dws[p, core, y] = (dws[p, core, y].astype(F32) + core_in[p, y].astype(F32)).astype(BF16)

    def dw_sum(p):
        v = dws[p, core, y].astype(F32)
        for j in range(3):
            dw_y(p, j).wait_recv()
            v = v + y_in[p, j].astype(F32)
        s2[p] = v.astype(BF16)

    def dw_z(i, way, step):
        return remote(z_out.at[i, way, step], z_in.at[i, way, step],
                      z_send.at[i, way, step], z_recv.at[i, way, step], (right, left)[way])

    def half(i):
        return slice(i * KEEP, (i + 1) * KEEP)

    def dw_ring(step):
        for i in range(2):
            for way in range(2):
                n = HOPS[i][way]
                if step >= n:
                    continue
                d = (z + n - step) % ZN if way == 0 else (z + ZN - n + step) % ZN
                if step == 0:
                    z_out[i, way, step] = s2[d, half(i)]
                else:
                    dw_z(i, way, step - 1).wait_recv()
                    v = s2[d, half(i)].astype(F32) + z_in[i, way, step - 1].astype(F32)
                    z_out[i, way, step] = v.astype(BF16)
                dw_z(i, way, step).start()

    xh_copy = remote(xh_out, xh_in, xh_send, xh_recv, xh_peer)

    def dw_to_x():
        for i in range(2):
            total = s2[z, half(i)].astype(F32)
            for way in range(2):
                dw_z(i, way, HOPS[i][way] - 1).wait_recv()
                total = total + z_in[i, way, HOPS[i][way] - 1].astype(F32)
            low, high = total[:, :8], total[:, 8:]
            dw_ref[half(i)] = jnp.where(xh == 0, low, high)
            xh_out[half(i)] = jnp.where(xh == 0, high, low)
        xh_copy.start()

    def dw_end():
        xh_copy.wait_recv()
        dw_ref[...] += xh_in[...]

    def when(cond, f):
        pl.when(cond)(f)

    def q_wait(g):
        for c in q_copies[g]:
            c.wait_recv()

    def x_ready():
        x_copy.wait_recv()
        turn_x(1 - h)

    def assemble(i, carry):
        zz, m = i // (TZ // 2), i % (TZ // 2)
        v = wg[:, :, zz, :, pl.ds(pl.multiple_of(m * 16, 16), 16), :].astype(F32).reshape(2, YN, 2, 2, 8, W)
        v = v.transpose(3, 1, 2, 0, 4, 5).reshape(2, W, W)
        wt[pl.ds(zz * TZ + m * 2, 2)] = v.astype(BF16)
        return carry

    def weights_ready():
        w_core.wait_recv()
        lax.fori_loop(0, ZN * TZ // 2, assemble, 0)

    plan = {
        1: [(ring_step, 1, 0, 0), (ring_step, 1, 1, 0)],
        2: [(w_step, 3)],
        3: [(q_wait, 0)],
        4: [(ring_step, 1, 0, 1), (ring_step, 1, 1, 1)],
        7: [(ring_step, 1, 0, 2), (ring_step, 1, 1, 2)],
        9: [(q_wait, 1), (w_pass,)],
        10: [(x_ready,), (dw_tiles, 0), (dw_tiles, 1)],
        11: [(ring_step, 1, 0, 3), (ring_step, 1, 1, 3)],
        12: [(rs_step, 0, 0), (turn_keys, 1), (dw_tiles, 2), (dw_tiles, 3)],
        13: [(dw_to_y, 0), (dw_to_y, 1)],
        15: [(q_wait, 2), (rs_step, 0, 1), (dw_to_y, 2), (dw_to_y, 3)],
        17: [(w_swap,)],
        18: [(rs_step, 0, 2), (dw_tiles, 4), (dw_tiles, 5)],
        21: [(q_wait, 3), (rs_step, 0, 3), (dw_to_y, 4), (dw_to_y, 5)],
    }

    def work(it, carry):
        def tick(phase):
            for slot, steps in plan.items():
                if slot % 3 == phase:

                    @pl.when(it == slot // 3)
                    def _():
                        for f, *rest in steps:
                            f(*rest)

        theirs, quarter = it % 2, it // 2
        attend(it // 4, jnp.where(theirs == 0, h, 1 - h), quarter * HP, z,
               qbuf, dobuf, kv, kt, acc, e_scr, dp_scr, q_s, do_s, dq_t, dq, tick)
        return carry

    lax.fori_loop(0, 8, work, 0)

    def dx_part(r2):
        part = cols(r2 * 2 * W, 2 * W)
        return remote(dx_out.at[:, part], dx_in.at[:, part], dx_send.at[r2], dx_recv.at[r2], partner)

    def dx_step(r2, carry):
        for i in range(2):
            for c in range(16):
                at = inv_ref[(r2 * 2 + i) * 16 + c]
                tile = wt[jnp.maximum(at, 0)]
                wcat[i * W : (i + 1) * W, c * W : (c + 1) * W] = jnp.where(at >= 0, tile, jnp.zeros_like(tile))
        part = cols(r2 * 2 * W, 2 * W)
        out = dot_t(dq[...].reshape(2 * W, HALF), wcat[...])
        first, second = out[:W], out[W:]
        dx_out[:, part] = jnp.where(h == 0, second, first).astype(BF16)
        dx_part(r2).start()
        dx_own[:, part] = jnp.where(h == 0, first, second)
        return carry

    def dx_end(r2, carry):
        dx_part(r2).wait_recv()
        part = cols(r2 * 2 * W, 2 * W)
        dx_ref[:, part] = (dx_own[:, part] + dx_in[:, part].astype(F32)).astype(BF16)
        return carry

    rs_step(1, 0)
    dw_tiles(6)
    dw_tiles(7)
    for p in range(4):
        dw_sum(p)
    dw_to_y(6)
    dw_to_y(7)
    rs_end(0)
    rs_step(1, 1)
    weights_ready()
    lax.fori_loop(0, 3, dx_step, 0)
    dw_sum(4)
    dw_sum(5)
    rs_step(1, 2)
    lax.fori_loop(3, 5, dx_step, 0)
    dw_sum(6)
    dw_sum(7)
    dw_ring(0)
    rs_step(1, 3)
    lax.fori_loop(5, 7, dx_step, 0)
    dw_ring(1)
    rs_end(1)
    lax.fori_loop(7, 9, dx_step, 0)
    dw_ring(2)
    lax.fori_loop(9, 10, dx_step, 0)
    rs_out(0)
    dw_ring(3)
    rs_out(1)
    dw_to_x()
    lax.fori_loop(0, 10, dx_end, 0)
    dw_end()

    for c in swaps[0] + swaps[1] + sum(q_copies, []) + [x_copy, wx, w_core, xh_copy]:
        c.wait_send()
    for way in range(2):
        for step in range(4):
            wring(way, step).wait_send()
            for i in range(2):
                if step < HOPS[i][way]:
                    ring(0, i, way, step).wait_send()
                    ring(1, i, way, step).wait_send()
        y_pass(way).wait_send()
    for g in range(2):
        for i in range(2):
            for way in range(2):
                for step in range(HOPS[i][way]):
                    rs(g, i, way, step).wait_send()
        pair(g).wait_send()

    def sent_w(i, carry):
        for j in range(2):
            to_y(i, j).wait_send()
        return carry

    lax.fori_loop(0, ZN, sent_w, 0)

    def sent_dw(p, carry):
        to_core(p).wait_send()
        for j in range(3):
            dw_y(p, j).wait_send()
        return carry

    lax.fori_loop(0, ZN, sent_dw, 0)
    for i in range(2):
        for way in range(2):
            for step in range(HOPS[i][way]):
                dw_z(i, way, step).wait_send()

    def sent_dx(r2, carry):
        dx_part(r2).wait_send()
        return carry

    lax.fori_loop(0, 10, sent_dx, 0)


def fused(rows, x, q, k, v, do, w):
    any_spec = pl.BlockSpec(memory_space=pl.ANY)
    vmem = pl.BlockSpec(memory_space=pltpu.VMEM)
    smem = pl.BlockSpec(memory_space=pltpu.SMEM)
    dma = pltpu.SemaphoreType.DMA

    def low(*shape):
        return pltpu.VMEM(shape, BF16)

    def full(*shape):
        return pltpu.VMEM(shape, F32)

    return pl.pallas_call(
        fused_kernel,
        out_shape=(
            jax.ShapeDtypeStruct((W, D), BF16),
            jax.ShapeDtypeStruct((W, 512), BF16),
            jax.ShapeDtypeStruct((W, 512), BF16),
            jax.ShapeDtypeStruct((TZ, 8, W), F32),
        ),
        in_specs=[smem] + [any_spec] * 6,
        out_specs=(vmem,) * 4,
        scratch_shapes=[
            low(2, W, HALF), low(2, W, HALF), low(2, 2, 2, ZN, W, W), low(2, W, 2048), full(2, 2, 2048, W),
            full(2048, R), full(2048, R), low(R, W), low(R, W), full(W, R), low(2, W, HALF),
            low(2, W, D), low(RTILES, 2, W, W), low(2, YN, ZN, 2, TZ * 8, W), low(ZN * TZ, W, W), low(2 * W, HALF),
            low(ZN, 2, YN, TZ, 16, W), low(ZN, YN, TZ, 16, W), low(ZN, 3, TZ, 16, W), low(ZN, TZ, 16, W),
            low(2, 2, 4, KEEP, 16, W), low(2, 2, 4, KEEP, 16, W), full(TZ, 8, W), full(TZ, 8, W),
            pltpu.SMEM((16,), jnp.int32), pltpu.SMEM((RTILES * 16,), jnp.int32), full(W, D), low(W, D), low(W, D),
            low(2, 4, 2, 2, W, W), low(2, 4, 2, 2, W, W), low(2, 4, 2, 2, W, W), low(2, 4, 2, 2, W, W),
            low(2, 2, W, W), low(2, 2, W, W),
            dma((10,)), dma((2, 2)), dma((2, 2)), dma((4, 2)), dma((4, 2)), dma, dma,
            dma((2, 2, 2, 4)), dma((2, 2, 2, 4)), dma, dma, dma((2, 4)), dma((2, 4)), dma((ZN, 2)), dma((ZN, 2)), dma((2,)), dma((2,)),
            dma, dma,
            dma((2, 2, 2, 4)), dma((2, 2, 2, 4)), dma((2,)), dma((2,)), dma((ZN,)), dma((ZN,)), dma((ZN, 3)), dma((ZN, 3)),
            dma((2, 2, 4)), dma((2, 2, 4)), dma, dma, dma((10,)), dma((10,)),
        ],
        compiler_params=pltpu.CompilerParams(
            collective_id=0, has_side_effects=True, vmem_limit_bytes=VMEM_LIMIT
        ),
        cost_estimate=pl.CostEstimate(flops=14 * 10**9, bytes_accessed=8 * 10**6, transcendentals=10**7),
    )(rows, x, q, k, v, do, w)


def body(x, q, k, v, do, w, tile_rows, loss_scale):
    dx, dk, dv, dw = fused(
        tile_rows, x[0], q[0], k[0], v[0], do[0], w.reshape(TZ * 8, W))
    return dx[None], dk[None], dv[None], dw / loss_scale[0].astype(F32)


def solution(mesh):
    tokens = P("dp", "seq", None)
    tiles = P("seq", "dp", None)
    return jax.shard_map(
        body,
        mesh=mesh,
        in_specs=(tokens,) * 5 + (tiles, P(), P()),
        out_specs=(tokens, tokens, tokens, tiles),
        check_vma=False,
    )
```

time: 137 us -> 115 us (0.84)
  the two profiles are of different devices: /device:TPU:248 before, /device:TPU:2 now
where the time goes in v3:
time: 115 us
  Pallas kernels  107 us (93%)
  local copies, waits for them, and re-layouts  4.99 us (4%)
  other arithmetic  1.54 us (1%)
  between operations  1.29 us (1%)
    pallas_call x1, Pallas kernels, fused(): pl.pallas_call(fused_kernel, out_shape=(jax.ShapeDtypeStruct((W, D), BF16...  107 us
    unnamed x8, local copies, waits for them, and re-layouts  4.99 us

profile of v3, /device:TPU:2, one launch (start us, length us, event | category | flops | bytes accessed | tf_op | source)
XLA Modules:
  0.0 115.1 jit_solution(15643901261956402423)
XLA Ops:
  0.6 1.4 %copy.12.rows_ref = s32[32,10]{1,0:T(8,128)} copy(s32[32,10]{0,1:T(8,128)} %param.14) | data formatting | bytes 2560 | tf_op args[6]
  2.0 107.3 %shard_map.111 = (bf16[128,2560]{1,0:T(8,128)(2,1)}, bf16[128,512]{1,0:T(8,128)(2,1)}, bf16[128,512]{1,0:T(8,128)(2,1)}, f32[20,8,128]{2,1,0:T(8,128)}) custom-call(s32[32,10]{1,0:T(8,128)} %copy.12.rows_ref, bf16[128,2560]{1,0:T(8,128)(2,1)} %bitcast.15, bf16[128,4096]{1,0:T(8,128)(2,1)} %bitcast.13, bf16[128,512]{1,0:T(8,128)(2,1)} %bitcast.16, ...), custom_call_target="tpu_custom_call" | custom-call | flops 14000000000 | bytes 8000000 | tf_op jit(solution)/shard_map/pallas_call | solution.py:566
  110.0 1.5 %broadcast_divide_fusion = f32[20,8,128]{2,1,0:T(8,128)} fusion(f32[20,8,128]{2,1,0:T(8,128)} %get-tuple-element.11, f32[]{:T(128)} %bitcast.9), kind=kLoop, calls=%fused_computation | loop fusion | flops 20480 | bytes 163844 | tf_op jit(solution)/shard_map/div | solution.py:601
  111.5 0.0 copy-start.1
  111.5 2.0 %copy.17 = bf16[1,128,2560]{2,1,0:T(8,128)(2,1)} copy(bf16[1,128,2560]{2,1,0:T(8,128)(2,1)} %bitcast.10) | data formatting | bytes 1310720
  113.5 0.0 copy-done.1
  113.5 0.0 copy-start
  113.5 0.7 copy.18
  114.2 0.3 copy-done
  114.5 0.7 copy.19
Async XLA Ops:
  111.5 2.0 %copy-start.1 = (bf16[128,512]{1,0:T(8,128)(2,1)S(1)}, bf16[128,512]{1,0:T(8,128)(2,1)}, u32[]{:S(2)}) copy-start(bf16[128,512]{1,0:T(8,128)(2,1)} %get-tuple-element.9) | copy-start | bytes 393220
  113.5 1.0 copy-start

commit v4 on v3

--- a/solution.py
+++ b/solution.py
@@ -15,7 +15,7 @@
 HALF = 2048
 HP = 4
 R = HP * W
-CK = 512
+CK = 1024
 KB = CK // W
 YN = 4
 HOPS = ((4, 3), (3, 4))
@@ -379,7 +379,8 @@
                     z_out[i, way, step] = v.astype(BF16)
                 dw_z(i, way, step).start()
 
-    xh_copy = remote(xh_out, xh_in, xh_send, xh_recv, xh_peer)
+    xh_copies = [remote(xh_out.at[pl.ds(i * KEEP, KEEP)], xh_in.at[pl.ds(i * KEEP, KEEP)],
+                        xh_send.at[i], xh_recv.at[i], xh_peer) for i in range(2)]
 
     def dw_to_x():
         for i in range(2):
@@ -390,11 +391,12 @@
             low, high = total[:, :8], total[:, 8:]
             dw_ref[half(i)] = jnp.where(xh == 0, low, high)
             xh_out[half(i)] = jnp.where(xh == 0, high, low)
-        xh_copy.start()
+            xh_copies[i].start()
 
     def dw_end():
-        xh_copy.wait_recv()
-        dw_ref[...] += xh_in[...]
+        for i in range(2):
+            xh_copies[i].wait_recv()
+            dw_ref[half(i)] += xh_in[half(i)]
 
     def when(cond, f):
         pl.when(cond)(f)
@@ -432,7 +434,8 @@
         15: [(q_wait, 2), (rs_step, 0, 1), (dw_to_y, 2), (dw_to_y, 3)],
         17: [(w_swap,)],
         18: [(rs_step, 0, 2), (dw_tiles, 4), (dw_tiles, 5)],
-        21: [(q_wait, 3), (rs_step, 0, 3), (dw_to_y, 4), (dw_to_y, 5)],
+        20: [(dw_to_y, 4), (dw_to_y, 5)],
+        21: [(q_wait, 3), (rs_step, 0, 3)],
     }
 
     def work(it, carry):
@@ -476,39 +479,38 @@
         dx_ref[:, part] = (dx_own[:, part] + dx_in[:, part].astype(F32)).astype(BF16)
         return carry
 
-    rs_step(1, 0)
     dw_tiles(6)
     dw_tiles(7)
+    rs_step(1, 0)
     for p in range(4):
         dw_sum(p)
     dw_to_y(6)
     dw_to_y(7)
     rs_end(0)
+    weights_ready()
     rs_step(1, 1)
-    weights_ready()
     lax.fori_loop(0, 3, dx_step, 0)
     dw_sum(4)
     dw_sum(5)
     rs_step(1, 2)
-    lax.fori_loop(3, 5, dx_step, 0)
     dw_sum(6)
     dw_sum(7)
     dw_ring(0)
+    lax.fori_loop(3, 5, dx_step, 0)
     rs_step(1, 3)
+    dw_ring(1)
     lax.fori_loop(5, 7, dx_step, 0)
-    dw_ring(1)
+    dw_ring(2)
     rs_end(1)
-    lax.fori_loop(7, 9, dx_step, 0)
-    dw_ring(2)
-    lax.fori_loop(9, 10, dx_step, 0)
+    lax.fori_loop(7, 10, dx_step, 0)
+    dw_ring(3)
     rs_out(0)
-    dw_ring(3)
     rs_out(1)
     dw_to_x()
     lax.fori_loop(0, 10, dx_end, 0)
     dw_end()
 
-    for c in swaps[0] + swaps[1] + sum(q_copies, []) + [x_copy, wx, w_core, xh_copy]:
+    for c in swaps[0] + swaps[1] + sum(q_copies, []) + xh_copies + [x_copy, wx, w_core]:
         c.wait_send()
     for way in range(2):
         for step in range(4):
@@ -586,7 +588,7 @@
             dma((2, 2, 2, 4)), dma((2, 2, 2, 4)), dma, dma, dma((2, 4)), dma((2, 4)), dma((ZN, 2)), dma((ZN, 2)), dma((2,)), dma((2,)),
             dma, dma,
             dma((2, 2, 2, 4)), dma((2, 2, 2, 4)), dma((2,)), dma((2,)), dma((ZN,)), dma((ZN,)), dma((ZN, 3)), dma((ZN, 3)),
-            dma((2, 2, 4)), dma((2, 2, 4)), dma, dma, dma((10,)), dma((10,)),
+            dma((2, 2, 4)), dma((2, 2, 4)), dma((2,)), dma((2,)), dma((10,)), dma((10,)),
         ],
         compiler_params=pltpu.CompilerParams(
             collective_id=0, has_side_effects=True, vmem_limit_bytes=VMEM_LIMIT

time: 115 us -> 114 us (level)
  Pallas kernels: 107 us -> 105 us
    pallas_call x1, Pallas kernels: 107 us -> 105 us  [fused(): pl.pallas_call(fused_kernel, out_shape=(jax.ShapeDtypeStruct((W, D), BF16...]
where the time goes in v4:
time: 114 us; the launch traced here: 113 us
  Pallas kernels  105 us (92%)
  local copies, waits for them, and re-layouts  4.99 us (4%)
  other arithmetic  1.54 us (1%)
  between operations  1.29 us (1%)
    pallas_call x1, Pallas kernels, fused(): pl.pallas_call(fused_kernel, out_shape=(jax.ShapeDtypeStruct((W, D), BF16...  105 us
    unnamed x8, local copies, waits for them, and re-layouts  4.99 us

profile of v4, /device:TPU:2, one launch (start us, length us, event | category | flops | bytes accessed | tf_op | source)
XLA Modules:
  0.0 113.0 jit_solution(5338635321344767521)
XLA Ops:
  0.6 1.4 %copy.12.rows_ref = s32[32,10]{1,0:T(8,128)} copy(s32[32,10]{0,1:T(8,128)} %param.14) | data formatting | bytes 2560 | tf_op args[6]
  2.0 105.2 %shard_map.111 = (bf16[128,2560]{1,0:T(8,128)(2,1)}, bf16[128,512]{1,0:T(8,128)(2,1)}, bf16[128,512]{1,0:T(8,128)(2,1)}, f32[20,8,128]{2,1,0:T(8,128)}) custom-call(s32[32,10]{1,0:T(8,128)} %copy.12.rows_ref, bf16[128,2560]{1,0:T(8,128)(2,1)} %bitcast.15, bf16[128,4096]{1,0:T(8,128)(2,1)} %bitcast.13, bf16[128,512]{1,0:T(8,128)(2,1)} %bitcast.16, ...), custom_call_target="tpu_custom_call" | custom-call | flops 14000000000 | bytes 8000000 | tf_op jit(solution)/shard_map/pallas_call | solution.py:568
  107.9 1.5 %broadcast_divide_fusion = f32[20,8,128]{2,1,0:T(8,128)} fusion(f32[20,8,128]{2,1,0:T(8,128)} %get-tuple-element.11, f32[]{:T(128)} %bitcast.9), kind=kLoop, calls=%fused_computation | loop fusion | flops 20480 | bytes 163844 | tf_op jit(solution)/shard_map/div | solution.py:603
  109.4 0.0 copy-start.1
  109.4 2.0 %copy.17 = bf16[1,128,2560]{2,1,0:T(8,128)(2,1)} copy(bf16[1,128,2560]{2,1,0:T(8,128)(2,1)} %bitcast.10) | data formatting | bytes 1310720
  111.4 0.0 copy-done.1
  111.4 0.0 copy-start
  111.4 0.7 copy.18
  112.1 0.3 copy-done
  112.4 0.7 copy.19
Async XLA Ops:
  109.4 2.0 %copy-start.1 = (bf16[128,512]{1,0:T(8,128)(2,1)S(1)}, bf16[128,512]{1,0:T(8,128)(2,1)}, u32[]{:S(2)}) copy-start(bf16[128,512]{1,0:T(8,128)(2,1)} %get-tuple-element.9) | copy-start | bytes 393220
  111.4 1.0 copy-start
